TPU v7x, 32 devices: a whole 2x2x4 slice. The times are simulated.
32 devices in a mesh: lat: 4 (over y, x), lon: 8 (over z, core).
Axes of the slice: x: 2, y: 2, z: 4, core: 2. Of those that a mesh axis runs over, the one named last changes fastest.
Arguments:
- target: float32 [3, 256, 4096], P(None, 'lat', 'lon'), may hold values from -8 to 8
- latent_0: float32 [256, 4096], P('lat', 'lon'), may hold values from -10 to 10
- latent_1: float32 [128, 2048], P('lat', 'lon'), may hold values from -10 to 10
- latent_2: float32 [64, 1024], P('lat', 'lon'), may hold values from -10 to 10
- latent_3: float32 [32, 512], P('lat', 'lon'), may hold values from -10 to 10
- latent_4: float32 [16, 256], P('lat', 'lon'), may hold values from -10 to 10
- latent_5: float32 [8, 128], P('lat', 'lon'), may hold values from -10 to 10
- tile_seeds: int32 [4, 8], P('lat', 'lon'), may hold values from 0 to 1073741823
- anchor_parity: int32 [6], replicated, may hold values from 0 to 1
- anchor_scale: float32 [6], replicated, may hold values from 0.5 to 4
- mix_levels: bfloat16 [24, 6], replicated, may hold values from -2.5 to 2.5
- mix_hidden: bfloat16 [24, 24], replicated, may hold values from -1.25 to 1.25
- conv_first: bfloat16 [24, 24, 3, 3], replicated, may hold values from -0.4375 to 0.4375
- conv_second: bfloat16 [24, 24, 3, 3], replicated, may hold values from -0.4375 to 0.4375
- conv_output: bfloat16 [3, 24, 3, 3], replicated, may hold values from -0.4375 to 0.4375
- context_in: float32 [24, 12], replicated, may hold values from -1.75 to 1.75
- context_mid: float32 [24, 24], replicated, may hold values from -1.25 to 1.25
- context_out: float32 [2, 24], replicated, may hold values from -1.25 to 1.25
Outputs:
- reconstruction: float32 [3, 256, 4096], P(None, 'lat', 'lon')
- bits_finest: float32 [256, 4096], P('lat', 'lon')
- loss_terms: float32 [7], replicated
- output_grad: float32 [3, 24, 3, 3], replicated
All inputs are finite; a program needn't handle non-finite values.
Results may differ from a plain program's by a relative error of at most 0.00035.
The roundings to bfloat16 on the way count: a program that leaves them out, or rounds other values in their place, can miss the bound.
Values may be sent and summed in bfloat16 or wider, within the bound.
A program may use at most 128 MiB of HBM per device.

v0:
```python
import jax
import jax.numpy as jnp
from jax import lax
from jax.sharding import PartitionSpec as P

mix_level = 668265263
mix_row = 374761393
mix_col = 1103515245
mix_mult = 73244475
log_two = 0.6931471805599453
context_steps = (
    (-1, 0),
    (1, 0),
    (0, -1),
    (0, 1),
    (-2, -1),
    (-2, 1),
    (2, -1),
    (2, 1),
    (-1, -2),
    (-1, 2),
    (1, -2),
    (1, 2),
)


def padded_2(shard, sides, width, wrap):
    for axis, dim in sides:
        size, length = (lax.axis_size(axis), shard.shape[dim])
        up = [(i, (i + 1) % size) for i in range(size if wrap else size - 1)]
        down = [(j, i) for i, j in up]
        last = lax.slice_in_dim(shard, length - width, length, axis=dim)
        first = lax.slice_in_dim(shard, 0, width, axis=dim)
        before = lax.ppermute(last, axis, up)
        after = lax.ppermute(first, axis, down)
        shard = jnp.concatenate([before, shard, after], axis=dim)
    return shard


def logical_shift(value, places):
    return jnp.bitwise_and(
        jnp.right_shift(value, jnp.int32(places)), jnp.int32((1 << 32 - places) - 1)
    )


def hashed_noise(seed_value, level_index, local_rows, local_cols):
    value = seed_value + jnp.int32(level_index) * jnp.int32(mix_level)
    value = (
        value + local_rows[:, None] * jnp.int32(mix_row) + local_cols[None, :] * jnp.int32(mix_col)
    )
    value = jnp.bitwise_xor(value, logical_shift(value, 15))
    value = value * jnp.int32(mix_mult)
    value = jnp.bitwise_xor(value, logical_shift(value, 13))
    value = value * jnp.int32(mix_mult)
    value = jnp.bitwise_xor(value, logical_shift(value, 16))
    return jnp.bitwise_and(value, jnp.int32(16777215)).astype(jnp.float32) / 16777216.0 - 0.5


def upsample_axis(extended, factor, along):
    cells_in = extended.shape[along] - 2
    earlier = lax.slice_in_dim(extended, 0, cells_in, axis=along)
    current = lax.slice_in_dim(extended, 1, cells_in + 1, axis=along)
    following = lax.slice_in_dim(extended, 2, cells_in + 2, axis=along)
    position = (jnp.arange(factor, dtype=jnp.float32) + 0.5) / factor - 0.5
    weight_low = jnp.maximum(-position, 0.0)
    weight_high = jnp.maximum(position, 0.0)
    weight_mid = 1.0 - weight_low - weight_high
    view_shape = [1] * (extended.ndim + 1)
    view_shape[along + 1] = factor
    result = jnp.expand_dims(earlier, along + 1) * weight_low.reshape(view_shape)
    result = result + jnp.expand_dims(current, along + 1) * weight_mid.reshape(view_shape)
    result = result + jnp.expand_dims(following, along + 1) * weight_high.reshape(view_shape)
    new_shape = list(extended.shape)
    new_shape[along] = cells_in * factor
    return result.reshape(new_shape)


def laplace_bits(offset, spread):
    magnitude = jnp.abs(offset)
    outer = (
        jnp.log(0.5)
        - (jnp.maximum(magnitude, 0.5) - 0.5) / spread
        + jnp.log(-jnp.expm1(-1.0 / spread))
    )
    inner_offset = jnp.clip(offset, -0.5, 0.5)
    inner = jnp.log(
        1.0
        - 0.5 * (jnp.exp(-(0.5 - inner_offset) / spread) + jnp.exp(-(0.5 + inner_offset) / spread))
    )
    return -jnp.where(magnitude >= 0.5, outer, inner) / log_two


def level_bits(
    extended, context_in, context_mid, context_out, anchor_value, parity_bit, row_start, col_start
):
    rows_in = extended.shape[0] - 4
    cols_in = extended.shape[1] - 4
    context = jnp.stack(
        [
            extended[2 + row_step : 2 + row_step + rows_in, 2 + col_step : 2 + col_step + cols_in]
            for row_step, col_step in context_steps
        ]
    )
    quantized = extended[2 : 2 + rows_in, 2 : 2 + cols_in]
    highest = lax.Precision.HIGHEST
    inner = jax.nn.relu(jnp.einsum("hk,kyx->hyx", context_in, context, precision=highest))
    outer = jax.nn.relu(jnp.einsum("hg,gyx->hyx", context_mid, inner, precision=highest))
    raw_out = jnp.einsum("oh,hyx->oyx", context_out, outer, precision=highest)
    row_ids = row_start + jnp.arange(rows_in, dtype=jnp.int32)
    col_ids = col_start + jnp.arange(cols_in, dtype=jnp.int32)
    anchor = (row_ids[:, None] + col_ids[None, :] + parity_bit) % 2 == 0
    centre = jnp.where(anchor, 0.0, raw_out[0])
    spread = jnp.where(anchor, anchor_value, 0.1 + jax.nn.softplus(raw_out[1]))
    return laplace_bits(quantized - centre, spread)


def conv_valid(field, kernel):
    return lax.conv_general_dilated(
        field[None],
        kernel,
        (1, 1),
        ((0, 0), (0, 0)),
        dimension_numbers=("NCHW", "OIHW", "NCHW"),
        preferred_element_type=jnp.float32,
    )[0]


def local(
    target,
    latent_0,
    latent_1,
    latent_2,
    latent_3,
    latent_4,
    latent_5,
    tile_seeds,
    anchor_parity,
    anchor_scale,
    mix_levels,
    mix_hidden,
    conv_first,
    conv_second,
    conv_output,
    context_in,
    context_mid,
    context_out,
):
    lat_count = lax.axis_size("lat")
    lon_count = lax.axis_size("lon")
    lat_index = lax.axis_index("lat")
    lon_index = lax.axis_index("lon")
    rows_dev = target.shape[1]
    cols_dev = target.shape[2]
    band_rows = rows_dev * lat_count
    latents = (latent_0, latent_1, latent_2, latent_3, latent_4, latent_5)
    seed_value = tile_seeds[0, 0]
    noisy = []
    for level_index, latent in enumerate(latents):
        rows_here, cols_here = latent.shape
        noise = hashed_noise(
            seed_value,
            level_index,
            jnp.arange(rows_here, dtype=jnp.int32),
            jnp.arange(cols_here, dtype=jnp.int32),
        )
        noisy.append(latent + noise)
    level_count = len(noisy)
    halo_widths = [
        max(2, (3 + 2**level_index - 1) // 2**level_index + 1) for level_index in range(level_count)
    ]
    extended = []
    for field, width in zip(noisy, halo_widths):
        sideways = padded_2(field, (("lon", 1),), width, True)
        extended.append(padded_2(sideways, (("lat", 0),), width, False))

    def inside(field, margin):
        row_ids = lat_index * rows_dev - margin + jnp.arange(field.shape[1], dtype=jnp.int32)
        keep = (row_ids >= 0) & (row_ids < band_rows)
        return jnp.where(keep[None, :, None], field, jnp.zeros_like(field))

    bit_sums = []
    cell_counts = []
    bits_finest = None
    for level_index, field in enumerate(extended):
        rows_here, cols_here = noisy[level_index].shape
        extra = halo_widths[level_index] - 2
        near = field[extra : field.shape[0] - extra, extra : field.shape[1] - extra]
        bits = level_bits(
            near,
            context_in,
            context_mid,
            context_out,
            anchor_scale[level_index],
            anchor_parity[level_index],
            lat_index * rows_here,
            lon_index * cols_here,
        )
        if level_index == 0:
            bits_finest = bits
        bit_sums.append(jnp.sum(bits))
        cell_counts.append(float(rows_here * cols_here * lat_count * lon_count))
    rate_local = jnp.stack(bit_sums)
    up_layers = []
    for level_index, field in enumerate(extended):
        factor = 2**level_index
        spare = (3 + factor - 1) // factor
        window = field
        grown = upsample_axis(upsample_axis(window, factor, 0), factor, 1)
        margin = spare * factor - 3
        up_layers.append(grown[margin : margin + rows_dev + 6, margin : margin + cols_dev + 6])
    upsampled = jnp.stack(up_layers).astype(jnp.bfloat16)
    first = jax.nn.relu(
        jnp.einsum("cl,lhw->chw", mix_levels, upsampled, preferred_element_type=jnp.float32)
    ).astype(jnp.bfloat16)
    second = jax.nn.relu(
        jnp.einsum("cd,dhw->chw", mix_hidden, first, preferred_element_type=jnp.float32)
    ).astype(jnp.bfloat16)
    deeper = inside(second, 3)
    third = inside(
        (deeper[:, 1:-1, 1:-1] + jax.nn.relu(conv_valid(deeper, conv_first))).astype(jnp.bfloat16),
        2,
    )
    fourth = inside(
        (third[:, 1:-1, 1:-1] + jax.nn.relu(conv_valid(third, conv_second))).astype(jnp.bfloat16), 1
    )
    reconstruction = conv_valid(fourth, conv_output)
    pixel_count = float(target.shape[0] * rows_dev * cols_dev * lat_count * lon_count)
    error = reconstruction - target
    squared_local = jnp.sum(error * error)
    slope = (2.0 * error / pixel_count).astype(jnp.bfloat16)
    taps = []
    for row_tap in range(3):
        for col_tap in range(3):
            window = fourth[:, row_tap : row_tap + rows_dev, col_tap : col_tap + cols_dev]
            taps.append(
                jnp.einsum("ohw,chw->oc", slope, window, preferred_element_type=jnp.float32)
            )
    grad_local = jnp.stack(taps, axis=-1).reshape(target.shape[0], second.shape[0], 3, 3)
    rate_total, squared_total, grad_total = lax.psum(
        (rate_local, squared_local, grad_local), ("lat", "lon")
    )
    cells = jnp.array(cell_counts, dtype=jnp.float32)
    loss_terms = jnp.concatenate([squared_total[None] / pixel_count, rate_total / cells])
    return (reconstruction, bits_finest, loss_terms, grad_total)


def solution(mesh):
    return jax.shard_map(
        local,
        mesh=mesh,
        in_specs=(
            P(None, "lat", "lon"),
            P("lat", "lon"),
            P("lat", "lon"),
            P("lat", "lon"),
            P("lat", "lon"),
            P("lat", "lon"),
            P("lat", "lon"),
            P("lat", "lon"),
            P(),
            P(),
            P(),
            P(),
            P(),
            P(),
            P(),
            P(),
            P(),
            P(),
        ),
        out_specs=(P(None, "lat", "lon"), P("lat", "lon"), P(), P()),
        check_vma=False,
    )
```

profile of v0, /device:TPU:0, one launch (start us, length us, event | category | flops | bytes accessed | tf_op | source)
XLA Modules:
  0.0 524.6 jit_solution(16472635620689725579)
XLA Ops:
  2.7 4.1 collective-permute-start.21
  35.6 4.5 collective-permute-start.22
  40.3 4.8 collective-permute-start.18
  54.9 4.3 collective-permute-start.14
  64.6 4.5 collective-permute-start.10
  70.7 4.9 collective-permute-start.6
  81.3 5.5 %collective-permute-start.2 = (f32[4,520]{1,0:T(4,128)S(1)}, f32[4,520]{1,0:T(4,128)S(1)}, u32[]{:S(2)}, u32[]{:S(2)}) collective-permute-start(f32[4,520]{1,0:T(4,128)S(1)} %get-tuple-element.13), channel_id=1, source_target_pairs={{0,8},{8,16},{16,24},{1,9},{9,17},{17,25},{2,10},{10,18},{18,26},{... | collective-permute-start | bytes 24968 | tf_op jit(solution)/shard_map/ppermute | solution.py:34
  110.2 5.4 %stack.327 = f32[12,64,512]{2,0,1:T(8,128)S(1)} concatenate(f32[1,64,512]{2,0,1:T(1,128)} %copy.487, f32[1,64,512]{2,0,1:T(1,128)} %copy.488, f32[1,64,512]{2,0,1:T(1,128)S(1)} %copy.489, f32[1,64,512]{2,0,1:T(1,128)S(1)} %copy.490, f32[1,64,512]{2,0,1:T(1,128)} %copy.491, f32[1,64,512]{2,0,1:T(1,128)} %copy.492, f32[1,64,512]{2,0,1:T(1,128)} %copy.493, ...), dimensions={0} | concatenate | bytes 3145728 | tf_op jit(solution)/shard_map/stack | solution.py:98
  132.3 5.4 %reshape.452 = bf16[24,70,1,8,65]{4,3,0,1,2:T(8,128)(2,1)S(1)} reshape(bf16[24,70,1,520]{3,0,1,2:T(8,128)(2,1)} %pad) | data formatting | bytes 3494400 | tf_op jit(solution)/shard_map/conv_general_dilated | solution.py:118
  137.8 8.6 %copy.478 = bf16[24,70,1,8,65]{0,3,4,1,2:T(8,128)(2,1)} copy(bf16[24,70,1,8,65]{4,3,0,1,2:T(8,128)(2,1)S(1)} %reshape.452) | data formatting | bytes 3494400 | tf_op jit(solution)/shard_map/conv_general_dilated | solution.py:118
  147.4 16.8 %select_maximum_fusion = f32[68,8,65,24]{3,1,2,0:T(8,128)} fusion(pred[8,65]{0,1:T(8,128)(4,1)S(1)} %copy-done.26, bf16[24,24,3,3]{1,0,3,2:T(8,128)(2,1)S(1)} %copy-done, bf16[24,70,1,7,2]{0,3,4,1,2:T(8,128)(2,1)S(1)} %slice.840, bf16[24,70,1,8,65]{0,3,4,1,2:T(8,128)(2,1)} %copy.478), kind=kOutput, calls=%fused_computation.6 | convolution fusion | flops 373712640 | bytes 5199688 | tf_op jit(solution)/shard_map/conv_general_dilated | solution.py:118
  164.2 14.0 %copy.479 = f32[68,8,65,24]{2,1,3,0:T(8,128)} copy(f32[68,8,65,24]{3,1,2,0:T(8,128)} %select_maximum_fusion) | data formatting | bytes 6789120 | tf_op jit(solution)/shard_map/jit(relu)/max | solution.py:220
  178.3 7.3 %reshape.456 = f32[68,1,520,24]{2,3,0,1:T(8,128)} reshape(f32[68,8,65,24]{2,1,3,0:T(8,128)} %copy.479) | data formatting | bytes 6789120 | tf_op jit(solution)/shard_map/jit(relu)/max | solution.py:220
  185.6 4.3 fusion.46
  191.5 6.6 %reshape.459 = bf16[24,68,1,8,65]{4,3,0,1,2:T(8,128)(2,1)} reshape(bf16[24,68,1,520]{3,0,1,2:T(8,128)(2,1)} %pad.2) | data formatting | bytes 3394560 | tf_op jit(solution)/shard_map/conv_general_dilated | solution.py:118
  198.0 11.0 %copy.481 = bf16[24,68,1,8,65]{0,3,4,1,2:T(8,128)(2,1)} copy(bf16[24,68,1,8,65]{4,3,0,1,2:T(8,128)(2,1)} %reshape.459) | data formatting | bytes 3394560 | tf_op jit(solution)/shard_map/conv_general_dilated | solution.py:118
  210.1 16.4 %select_maximum_fusion.1 = f32[66,8,65,24]{3,1,2,0:T(8,128)} fusion(pred[8,65]{0,1:T(8,128)(4,1)S(1)} %copy-done.25, bf16[24,24,3,3]{1,0,3,2:T(8,128)(2,1)S(1)} %copy-done.19, bf16[24,68,1,7,2]{0,3,4,1,2:T(8,128)(2,1)S(1)} %slice.843, bf16[24,68,1,8,65]{0,3,4,1,2:T(8,128)(2,1)} %copy.481), kind=kOutput, calls=%fused_computation.7 | convolution fusion | flops 362725632 | bytes 5048584 | tf_op jit(solution)/shard_map/conv_general_dilated | solution.py:118
  226.5 13.7 %copy.482 = f32[66,8,65,24]{2,1,3,0:T(8,128)} copy(f32[66,8,65,24]{3,1,2,0:T(8,128)} %select_maximum_fusion.1) | data formatting | bytes 6589440 | tf_op jit(solution)/shard_map/jit(relu)/max | solution.py:224
  240.2 7.2 %reshape.463 = f32[66,1,520,24]{2,3,0,1:T(8,128)} reshape(f32[66,8,65,24]{2,1,3,0:T(8,128)} %copy.482) | data formatting | bytes 6589440 | tf_op jit(solution)/shard_map/jit(relu)/max | solution.py:224
  253.8 5.2 reshape.466
  259.0 8.4 %copy.484 = bf16[24,66,1,8,65]{0,3,4,1,2:T(8,128)(2,1)} copy(bf16[24,66,1,8,65]{4,3,0,1,2:T(8,128)(2,1)S(1)} %reshape.466) | data formatting | bytes 3294720 | tf_op jit(solution)/shard_map/conv_general_dilated | solution.py:118
  268.5 190.7 %fusion.31 = f32[64,8,65,3]{1,3,2,0:T(4,128)} fusion(bf16[24,66,1,7,2]{0,3,4,1,2:T(8,128)(2,1)S(1)} %slice.845, bf16[24,66,1,8,65]{0,3,4,1,2:T(8,128)(2,1)} %copy.484, pred[8,65]{0,1:T(8,128)(4,1)S(1)} %copy-done.24, bf16[3,24,3,3]{1,3,2,0:T(4,128)(2,1)S(1)} %copy-done.20), kind=kOutput, calls=%fused_computation.29 | convolution fusion | flops 48324864 | bytes 2092888 | tf_op jit(solution)/shard_map/conv_general_dilated | solution.py:118
  459.2 6.0 %copy.486 = f32[64,8,65,3]{2,1,0,3:T(8,128)S(1)} copy(f32[64,8,65,3]{1,3,2,0:T(4,128)} %fusion.31) | data formatting | bytes 798720 | tf_op jit(solution)/shard_map/conv_general_dilated | solution.py:118
  482.9 40.3 %all-reduce = (f32[6]{0:T(128)S(1)}, f32[]{:T(128)}, f32[3,24,3,3]{1,3,2,0:T(4,128)}) all-reduce(f32[6]{0:T(128)S(1)} %stack.399, f32[]{:T(128)} %multiply_reduce_fusion, f32[3,24,3,3]{1,3,2,0:T(4,128)S(1)} %copy.568), channel_id=1, replica_groups=mesh['lat'=4,'lon'=8] {'lat','lon'}, use_global_device_ids=true, to_apply=%region_8.9 | all-reduce | flops 655 | bytes 5240 | tf_op jit(solution)/shard_map/psum | solution.py:239
  (434 shorter events, 120.6 us)
Async XLA Ops:
  2.2 20.4 %collective-permute-start.20 = (f32[2,2]{1,0:T(2,128)S(1)}, f32[2,2]{1,0:T(2,128)S(1)}, u32[]{:S(2)}, u32[]{:S(2)}) collective-permute-start(f32[2,2]{1,0:T(2,128)S(1)} %get-tuple-element.139), channel_id=1, source_target_pairs={{0,1},{1,2},{2,3},{3,4},{4,5},{5,6},{6,7},{7,0},{8,9},{9,10},{10,1... | collective-permute-start | bytes 56 | tf_op jit(solution)/shard_map/ppermute | solution.py:34
  2.7 23.5 %collective-permute-start.21 = (f32[2,2]{1,0:T(2,128)S(1)}, f32[2,2]{1,0:T(2,128)S(1)}, u32[]{:S(2)}, u32[]{:S(2)}) collective-permute-start(f32[2,2]{1,0:T(2,128)S(1)} %get-tuple-element.140), channel_id=1, source_target_pairs={{1,0},{2,1},{3,2},{4,3},{5,4},{6,5},{7,6},{0,7},{9,8},{10,9},{11,1... | collective-permute-start | bytes 56 | tf_op jit(solution)/shard_map/ppermute | solution.py:35
  7.6 19.0 %collective-permute-start.16 = (f32[4,2]{1,0:T(4,128)S(1)}, f32[4,2]{1,0:T(4,128)S(1)}, u32[]{:S(2)}, u32[]{:S(2)}) collective-permute-start(f32[4,2]{1,0:T(4,128)S(1)} %get-tuple-element.131), channel_id=1, source_target_pairs={{0,1},{1,2},{2,3},{3,4},{4,5},{5,6},{6,7},{7,0},{8,9},{9,10},{10,1... | collective-permute-start | bytes 104 | tf_op jit(solution)/shard_map/ppermute | solution.py:34
  7.6 22.5 %collective-permute-start.17 = (f32[4,2]{1,0:T(4,128)S(1)}, f32[4,2]{1,0:T(4,128)S(1)}, u32[]{:S(2)}, u32[]{:S(2)}) collective-permute-start(f32[4,2]{1,0:T(4,128)S(1)} %get-tuple-element.132), channel_id=1, source_target_pairs={{1,0},{2,1},{3,2},{4,3},{5,4},{6,5},{7,6},{0,7},{9,8},{10,9},{11,1... | collective-permute-start | bytes 104 | tf_op jit(solution)/shard_map/ppermute | solution.py:35
  12.0 18.5 %collective-permute-start.12 = (f32[8,2]{1,0:T(8,128)S(1)}, f32[8,2]{1,0:T(8,128)S(1)}, u32[]{:S(2)}, u32[]{:S(2)}) collective-permute-start(f32[8,2]{1,0:T(8,128)S(1)} %get-tuple-element.115), channel_id=1, source_target_pairs={{0,1},{1,2},{2,3},{3,4},{4,5},{5,6},{6,7},{7,0},{8,9},{9,10},{10,1... | collective-permute-start | bytes 200 | tf_op jit(solution)/shard_map/ppermute | solution.py:34
  22.7 11.4 %collective-permute-start.13 = (f32[8,2]{1,0:T(8,128)S(1)}, f32[8,2]{1,0:T(8,128)S(1)}, u32[]{:S(2)}, u32[]{:S(2)}) collective-permute-start(f32[8,2]{1,0:T(8,128)S(1)} %get-tuple-element.116), channel_id=1, source_target_pairs={{1,0},{2,1},{3,2},{4,3},{5,4},{6,5},{7,6},{0,7},{9,8},{10,9},{11,1... | collective-permute-start | bytes 200 | tf_op jit(solution)/shard_map/ppermute | solution.py:35
  26.2 8.1 %collective-permute-start.8 = (f32[16,2]{1,0:T(8,128)S(1)}, f32[16,2]{1,0:T(8,128)S(1)}, u32[]{:S(2)}, u32[]{:S(2)}) collective-permute-start(f32[16,2]{1,0:T(8,128)S(1)} %get-tuple-element.95), channel_id=1, source_target_pairs={{0,1},{1,2},{2,3},{3,4},{4,5},{5,6},{6,7},{7,0},{8,9},{9,10},{10,1... | collective-permute-start | bytes 392 | tf_op jit(solution)/shard_map/ppermute | solution.py:34
  26.6 9.0 %collective-permute-start.9 = (f32[16,2]{1,0:T(8,128)S(1)}, f32[16,2]{1,0:T(8,128)S(1)}, u32[]{:S(2)}, u32[]{:S(2)}) collective-permute-start(f32[16,2]{1,0:T(8,128)S(1)} %get-tuple-element.96), channel_id=1, source_target_pairs={{1,0},{2,1},{3,2},{4,3},{5,4},{6,5},{7,6},{0,7},{9,8},{10,9},{11,1... | collective-permute-start | bytes 392 | tf_op jit(solution)/shard_map/ppermute | solution.py:35
  30.2 33.1 %collective-permute-start.4 = (f32[32,3]{1,0:T(8,128)S(1)}, f32[32,3]{1,0:T(8,128)S(1)}, u32[]{:S(2)}, u32[]{:S(2)}) collective-permute-start(f32[32,3]{1,0:T(8,128)S(1)} %get-tuple-element.60), channel_id=1, source_target_pairs={{0,1},{1,2},{2,3},{3,4},{4,5},{5,6},{6,7},{7,0},{8,9},{9,10},{10,1... | collective-permute-start | bytes 1160 | tf_op jit(solution)/shard_map/ppermute | solution.py:34
  30.5 34.1 %collective-permute-start.5 = (f32[32,3]{1,0:T(8,128)S(1)}, f32[32,3]{1,0:T(8,128)S(1)}, u32[]{:S(2)}, u32[]{:S(2)}) collective-permute-start(f32[32,3]{1,0:T(8,128)S(1)} %get-tuple-element.61), channel_id=1, source_target_pairs={{1,0},{2,1},{3,2},{4,3},{5,4},{6,5},{7,6},{0,7},{9,8},{10,9},{11,1... | collective-permute-start | bytes 1160 | tf_op jit(solution)/shard_map/ppermute | solution.py:35
  34.0 45.9 %collective-permute-start = (f32[64,4]{1,0:T(8,128)S(1)}, f32[64,4]{1,0:T(8,128)S(1)}, u32[]{:S(2)}, u32[]{:S(2)}) collective-permute-start(f32[64,4]{1,0:T(8,128)S(1)} %get-tuple-element.27), channel_id=1, source_target_pairs={{0,1},{1,2},{2,3},{3,4},{4,5},{5,6},{6,7},{7,0},{8,9},{9,10},{10,1... | collective-permute-start | bytes 3080 | tf_op jit(solution)/shard_map/ppermute | solution.py:34
  34.3 6.0 %collective-permute-start.23 = (f32[2,20]{1,0:T(2,128)S(1)}, f32[2,20]{1,0:T(2,128)S(1)}, u32[]{:S(2)}, u32[]{:S(2)}) collective-permute-start(f32[2,20]{1,0:T(2,128)S(1)} %pad_maximum_fusion.39), channel_id=1, source_target_pairs={{8,0},{16,8},{24,16},{9,1},{17,9},{25,17},{10,2},{18,10},{26,18},{... | collective-permute-start | bytes 488 | tf_op jit(solution)/shard_map/ppermute | solution.py:35
  35.6 9.5 %collective-permute-start.22 = (f32[2,20]{1,0:T(2,128)S(1)}, f32[2,20]{1,0:T(2,128)S(1)}, u32[]{:S(2)}, u32[]{:S(2)}) collective-permute-start(f32[2,20]{1,0:T(2,128)S(1)} %pad_maximum_fusion.39), channel_id=1, source_target_pairs={{0,8},{8,16},{16,24},{1,9},{9,17},{17,25},{2,10},{10,18},{18,26},{... | collective-permute-start | bytes 488 | tf_op jit(solution)/shard_map/ppermute | solution.py:34
  40.3 11.8 %collective-permute-start.18 = (f32[2,36]{1,0:T(2,128)S(1)}, f32[2,36]{1,0:T(2,128)S(1)}, u32[]{:S(2)}, u32[]{:S(2)}) collective-permute-start(f32[2,36]{1,0:T(2,128)S(1)} %get-tuple-element.129), channel_id=1, source_target_pairs={{0,8},{8,16},{16,24},{1,9},{9,17},{17,25},{2,10},{10,18},{18,26},{... | collective-permute-start | bytes 872 | tf_op jit(solution)/shard_map/ppermute | solution.py:34
  45.1 9.8 %collective-permute-start.19 = (f32[2,36]{1,0:T(2,128)S(1)}, f32[2,36]{1,0:T(2,128)S(1)}, u32[]{:S(2)}, u32[]{:S(2)}) collective-permute-start(f32[2,36]{1,0:T(2,128)S(1)} %get-tuple-element.130), channel_id=1, source_target_pairs={{8,0},{16,8},{24,16},{9,1},{17,9},{25,17},{10,2},{18,10},{26,18},{... | collective-permute-start | bytes 872 | tf_op jit(solution)/shard_map/ppermute | solution.py:35
  52.1 29.1 %collective-permute-start.1 = (f32[64,4]{1,0:T(8,128)S(1)}, f32[64,4]{1,0:T(8,128)S(1)}, u32[]{:S(2)}, u32[]{:S(2)}) collective-permute-start(f32[64,4]{1,0:T(8,128)S(1)} %get-tuple-element.28), channel_id=1, source_target_pairs={{1,0},{2,1},{3,2},{4,3},{5,4},{6,5},{7,6},{0,7},{9,8},{10,9},{11,1... | collective-permute-start | bytes 3080 | tf_op jit(solution)/shard_map/ppermute | solution.py:35
  54.9 14.5 %collective-permute-start.14 = (f32[2,68]{1,0:T(2,128)S(1)}, f32[2,68]{1,0:T(2,128)S(1)}, u32[]{:S(2)}, u32[]{:S(2)}) collective-permute-start(f32[2,68]{1,0:T(2,128)S(1)} %get-tuple-element.113), channel_id=1, source_target_pairs={{0,8},{8,16},{16,24},{1,9},{9,17},{17,25},{2,10},{10,18},{18,26},{... | collective-permute-start | bytes 1640 | tf_op jit(solution)/shard_map/ppermute | solution.py:34
  63.3 7.4 %collective-permute-start.15 = (f32[2,68]{1,0:T(2,128)S(1)}, f32[2,68]{1,0:T(2,128)S(1)}, u32[]{:S(2)}, u32[]{:S(2)}) collective-permute-start(f32[2,68]{1,0:T(2,128)S(1)} %get-tuple-element.114), channel_id=1, source_target_pairs={{8,0},{16,8},{24,16},{9,1},{17,9},{25,17},{10,2},{18,10},{26,18},{... | collective-permute-start | bytes 1640 | tf_op jit(solution)/shard_map/ppermute | solution.py:35
  64.6 22.7 %collective-permute-start.10 = (f32[2,132]{1,0:T(2,128)S(1)}, f32[2,132]{1,0:T(2,128)S(1)}, u32[]{:S(2)}, u32[]{:S(2)}) collective-permute-start(f32[2,132]{1,0:T(2,128)S(1)} %get-tuple-element.75), channel_id=1, source_target_pairs={{0,8},{8,16},{16,24},{1,9},{9,17},{17,25},{2,10},{10,18},{18,26},{... | collective-permute-start | bytes 3176 | tf_op jit(solution)/shard_map/ppermute | solution.py:34
  69.4 19.3 %collective-permute-start.11 = (f32[2,132]{1,0:T(2,128)S(1)}, f32[2,132]{1,0:T(2,128)S(1)}, u32[]{:S(2)}, u32[]{:S(2)}) collective-permute-start(f32[2,132]{1,0:T(2,128)S(1)} %get-tuple-element.76), channel_id=1, source_target_pairs={{8,0},{16,8},{24,16},{9,1},{17,9},{25,17},{10,2},{18,10},{26,18},{... | collective-permute-start | bytes 3176 | tf_op jit(solution)/shard_map/ppermute | solution.py:35
  70.7 23.4 %collective-permute-start.6 = (f32[3,262]{1,0:T(4,128)S(1)}, f32[3,262]{1,0:T(4,128)S(1)}, u32[]{:S(2)}, u32[]{:S(2)}) collective-permute-start(f32[3,262]{1,0:T(4,128)S(1)} %get-tuple-element.37), channel_id=1, source_target_pairs={{0,8},{8,16},{16,24},{1,9},{9,17},{17,25},{2,10},{10,18},{18,26},{... | collective-permute-start | bytes 9440 | tf_op jit(solution)/shard_map/ppermute | solution.py:34
  80.0 14.2 %collective-permute-start.7 = (f32[3,262]{1,0:T(4,128)S(1)}, f32[3,262]{1,0:T(4,128)S(1)}, u32[]{:S(2)}, u32[]{:S(2)}) collective-permute-start(f32[3,262]{1,0:T(4,128)S(1)} %get-tuple-element.38), channel_id=1, source_target_pairs={{8,0},{16,8},{24,16},{9,1},{17,9},{25,17},{10,2},{18,10},{26,18},{... | collective-permute-start | bytes 9440 | tf_op jit(solution)/shard_map/ppermute | solution.py:35
  81.3 21.1 %collective-permute-start.2 = (f32[4,520]{1,0:T(4,128)S(1)}, f32[4,520]{1,0:T(4,128)S(1)}, u32[]{:S(2)}, u32[]{:S(2)}) collective-permute-start(f32[4,520]{1,0:T(4,128)S(1)} %get-tuple-element.13), channel_id=1, source_target_pairs={{0,8},{8,16},{16,24},{1,9},{9,17},{17,25},{2,10},{10,18},{18,26},{... | collective-permute-start | bytes 24968 | tf_op jit(solution)/shard_map/ppermute | solution.py:34
  87.3 15.2 %collective-permute-start.3 = (f32[4,520]{1,0:T(4,128)S(1)}, f32[4,520]{1,0:T(4,128)S(1)}, u32[]{:S(2)}, u32[]{:S(2)}) collective-permute-start(f32[4,520]{1,0:T(4,128)S(1)} %get-tuple-element.14), channel_id=1, source_target_pairs={{8,0},{16,8},{24,16},{9,1},{17,9},{25,17},{10,2},{18,10},{26,18},{... | collective-permute-start | bytes 24968 | tf_op jit(solution)/shard_map/ppermute | solution.py:35
  (27 other events, 607.8 us)
where the time goes:
time: 535 us; the launch traced here: 525 us
  matrix products  246 us (46%)
  local copies, waits for them, and re-layouts  142 us (27%)
  starting transfers between devices  57.9 us (11%)
  blocking collectives  40.3 us (8%)
  other arithmetic  34.9 us (7%)
    conv_general_dilated x3, matrix products, conv_valid(): lax.conv_general_dilated(field[None], kernel, (1, 1), ((0, 0), (0, 0)), d...  224 us
    conv_general_dilated x11, local copies, waits for them, and re-layouts, conv_valid(): lax.conv_general_dilated(field[None], kernel, (1, 1), ((0, 0), (0, 0)), d...  54.5 us
    psum x1, blocking collectives, local(): lax.psum((rate_local, squared_local, grad_local), ('lat', 'lon'))  40.3 us
    ppermute x12, starting transfers between devices, padded_2(): before = lax.ppermute(last, axis, up)  29 us
    ppermute x12, starting transfers between devices, padded_2(): after = lax.ppermute(first, axis, down)  28.9 us
    max x2, local copies, waits for them, and re-layouts, local(): jax.nn.relu(conv_valid(deeper, conv_first))  21.4 us
    max x2, local copies, waits for them, and re-layouts, local(): jax.nn.relu(conv_valid(third, conv_second))  21 us
    another operation x48, local copies, waits for them, and re-layouts, level_bits(): jnp.stack([extended[2 + row_step:2 + row_step + rows_in, 2 + col_step:2 +...  14.7 us
  transfers between devices with their start and end apart: 24, of which 0 were waited for; matrix products, arithmetic and copies ran while one was open for 8% of the time, Pallas kernels for 0%

commit v1 on v0

v1 whole, which is shorter than its diff:
```python
import functools

import jax
import jax.numpy as jnp
from jax import lax
from jax.experimental import pallas as pl
from jax.experimental.pallas import tpu as pltpu
from jax.sharding import PartitionSpec as P

mix_level = 668265263
mix_row = 374761393
mix_col = 1103515245
mix_mult = 73244475
log_two = 0.6931471805599453
context_steps = (
    (-1, 0),
    (1, 0),
    (0, -1),
    (0, 1),
    (-2, -1),
    (-2, 1),
    (2, -1),
    (2, 1),
    (-1, -2),
    (-1, 2),
    (1, -2),
    (1, 2),
)
MESH = pl.DeviceIdType.MESH
BF = jnp.bfloat16
F32 = jnp.float32
LANES = 128
SUB = 8


def width_of(cols):
    return cols + LANES if cols >= LANES else LANES


def iota(shape, dim):
    return lax.broadcasted_iota(jnp.int32, shape, dim)


def hashed_noise(seed_value, level_index, shape):
    value = seed_value + jnp.int32(level_index * mix_level % (1 << 32) - (1 << 32) * ((level_index * mix_level % (1 << 32)) >> 31))
    value = value + iota(shape, 0) * jnp.int32(mix_row) + iota(shape, 1) * jnp.int32(mix_col)
    value = value ^ lax.shift_right_logical(value, jnp.full(shape, 15, jnp.int32))
    value = value * jnp.int32(mix_mult)
    value = value ^ lax.shift_right_logical(value, jnp.full(shape, 13, jnp.int32))
    value = value * jnp.int32(mix_mult)
    value = value ^ lax.shift_right_logical(value, jnp.full(shape, 16, jnp.int32))
    return (value & jnp.int32(16777215)).astype(F32) / 16777216.0 - 0.5


def halo_kernel(shapes, seed_ref, *refs):
    n = len(shapes)
    latents, ext = refs[:n], refs[n : 2 * n]
    send_l, send_r, recv_r, recv_l, send_u, send_d, recv_b, recv_t, ssem, rsem = refs[2 * n :]
    lat, lon = lax.axis_index("lat"), lax.axis_index("lon")
    lats, lons = lax.axis_size("lat"), lax.axis_size("lon")
    left, right = (lat, lax.rem(lon + lons - 1, lons)), (lat, lax.rem(lon + 1, lons))
    up, down = (lax.rem(lat + lats - 1, lats), lon), (lax.rem(lat + 1, lats), lon)
    barrier = pltpu.get_barrier_semaphore()
    for other in (left, right, up, down):
        pl.semaphore_signal(barrier, inc=1, device_id=other, device_id_type=MESH)
    seed = seed_ref[0, 0]
    row = 0
    for level, (rows, cols) in enumerate(shapes):
        e = ext[level]
        tall = max(rows, SUB)
        e[...] = jnp.zeros_like(e)
        e[SUB : SUB + rows, 0:cols] = latents[level][...] + hashed_noise(seed, level, (rows, cols))
        if cols >= LANES:
            send_l[row : row + tall, :] = e[SUB : SUB + tall, 0:LANES]
            send_r[row : row + tall, :] = e[SUB : SUB + tall, cols - LANES : cols]
        else:
            whole = e[SUB : SUB + tall, :]
            send_l[row : row + tall, :] = whole
            send_r[row : row + tall, :] = pltpu.roll(whole, LANES - cols, 1)
        row += tall
    pl.semaphore_wait(barrier, 4)

    def copy(src, dst, index, other):
        return pltpu.make_async_remote_copy(
            src_ref=src,
            dst_ref=dst,
            send_sem=ssem.at[index],
            recv_sem=rsem.at[index],
            device_id=other,
            device_id_type=MESH,
        )

    to_left = copy(send_l, recv_r, 0, left)
    to_right = copy(send_r, recv_l, 1, right)
    to_left.start()
    to_right.start()
    to_left.wait()
    to_right.wait()
    row = 0
    lane0 = 0
    for level, (rows, cols) in enumerate(shapes):
        e = ext[level]
        tall = max(rows, SUB)
        from_right = recv_r[row : row + tall, :]
        from_left = recv_l[row : row + tall, :]
        lane = iota((tall, LANES), 1)
        if cols >= LANES:
            e[SUB : SUB + tall, cols : cols + LANES] = jnp.where(
                lane < LANES // 2, from_right, from_left
            )
        else:
            whole = e[SUB : SUB + tall, :]
            moved = pltpu.roll(from_right, cols, 1)
            halo = jnp.where(
                lane < cols + 4, moved, jnp.where(lane >= LANES - 4, from_left, 0.0)
            )
            e[SUB : SUB + tall, :] = jnp.where(lane < cols, whole, halo)
        wide = width_of(cols)
        send_u[:, lane0 : lane0 + wide] = e[SUB : 2 * SUB, :]
        send_d[:, lane0 : lane0 + wide] = e[tall : tall + SUB, :]
        row += tall
        lane0 += wide
    to_up = copy(send_u, recv_b, 2, up)
    to_down = copy(send_d, recv_t, 3, down)
    to_up.start()
    to_down.start()
    to_up.wait()
    to_down.wait()
    keep_t = jnp.where(lat > 0, 1.0, 0.0).astype(F32)
    keep_b = jnp.where(lat < lats - 1, 1.0, 0.0).astype(F32)
    lane0 = 0
    for level, (rows, cols) in enumerate(shapes):
        e = ext[level]
        wide = width_of(cols)
        top = recv_t[:, lane0 : lane0 + wide] * keep_t
        bottom = recv_b[:, lane0 : lane0 + wide] * keep_b
        reach = min(rows, SUB)
        e[SUB - reach : SUB, :] = top[:reach]
        e[SUB + rows : SUB + rows + reach, :] = bottom[:reach]
        lane0 += wide


def dot(a, b):
    return jnp.dot(a, b, preferred_element_type=F32)


def parts(x, count):
    out = []
    for _ in range(count):
        piece = x.astype(BF)
        out.append(piece)
        x = x - piece.astype(F32)
    return out


def dot_pairs(a, x):
    hi, lo = parts(x, 2)
    return dot(a[0], hi) + (dot(a[1], hi) + dot(a[0], lo))


def div_24(x):
    return (x * 2731) >> 16


def one_hot(flag):
    return jnp.where(flag, 1.0, 0.0).astype(BF)


def laplace_bits(offset, spread):
    magnitude = jnp.abs(offset)
    t = 1.0 / spread
    series = t * (1.0 - t * (0.5 - t * (1.0 / 6 - t * (1.0 / 24 - t * (1.0 / 120)))))
    gap = jnp.where(t < 0.1, series, 1.0 - jnp.exp(-t))
    outer = -log_two - (jnp.maximum(magnitude, 0.5) - 0.5) / spread + jnp.log(gap)
    inner_offset = jnp.clip(offset, -0.5, 0.5)
    inner = jnp.log(
        1.0
        - 0.5 * (jnp.exp(-(0.5 - inner_offset) / spread) + jnp.exp(-(0.5 + inner_offset) / spread))
    )
    return jnp.where(magnitude >= 0.5, outer, inner) * (-1.0 / log_two)


def local_kernel(shapes, ch, bands, pixel_count, *refs):
    n = len(shapes)
    ext = refs[:n]
    (
        target, parity, anchor, mix_l, mix_h, taps, c_in, c_mid, c_out,
        recon, bits_out, part, ups, second, third, fourth,
    ) = refs[n:]
    lat, lon = lax.axis_index("lat"), lax.axis_index("lon")
    lats = lax.axis_size("lat")
    rows_dev, cols_dev = shapes[0]
    wide = width_of(cols_dev)
    deep = SUB * ch
    reach = (SUB + 2) * ch
    stride = taps.shape[0] // 9

    lane_ch = iota((ch, deep), 1)
    fold = one_hot(lane_ch - ch * div_24(lane_ch) == iota((ch, deep), 0))
    same_row = div_24(iota((deep, deep), 0)) == div_24(iota((deep, deep), 1))

    def block_diagonal(w):
        return jnp.where(same_row, jnp.concatenate([dot(w, fold)] * SUB, 0), 0.0).astype(BF)

    def row_inside(w):
        k = w.shape[1]
        spread = one_hot((iota((k, k * SUB), 1) >> 3) == iota((k, k * SUB), 0))
        shape = (deep, k * SUB)
        keep = (iota(shape, 1) & 7) == div_24(iota(shape, 0))
        return jnp.where(keep, jnp.concatenate([dot(w, spread)] * SUB, 0), 0.0).astype(BF)

    def rows_out(w):
        wide_w = dot(w, fold)
        grown = jnp.concatenate(
            [jnp.broadcast_to(wide_w[o : o + 1], (SUB, deep)) for o in range(w.shape[0])], 0
        )
        shape = (w.shape[0] * SUB, deep)
        keep = (iota(shape, 0) & 7) == div_24(iota(shape, 1))
        return jnp.where(keep, grown, 0.0).astype(BF)

    t_levels = row_inside(mix_l[...])
    t_hidden = block_diagonal(mix_h[...])
    a_in = [row_inside(p) for p in parts(c_in[...], 2)]
    a_mid = [block_diagonal(p) for p in parts(c_mid[...], 2)]
    a_out = [rows_out(p) for p in parts(c_out[...], 2)]

    lane_re = iota((ch, reach), 1)
    fold_re = one_hot(lane_re - ch * div_24(lane_re) == iota((ch, reach), 0))
    wide_taps = dot(taps[...], fold_re)
    step = div_24(iota((deep, reach), 1)) - div_24(iota((deep, reach), 0))
    step_out = div_24(iota((bands * SUB, reach), 1)) - (iota((bands * SUB, reach), 0) & 7)

    def conv_taps(first_row):
        out = []
        for b in range(3):
            total = jnp.zeros((deep, reach), F32)
            for a in range(3):
                at = (3 * a + b) * stride + first_row
                total = jnp.where(
                    step == a, jnp.concatenate([wide_taps[at : at + ch]] * SUB, 0), total
                )
            out.append(total.astype(BF))
        return jnp.concatenate(out, 0)

    def output_taps():
        out = []
        for b in range(3):
            total = jnp.zeros((bands * SUB, reach), F32)
            for a in range(3):
                at = (3 * a + b) * stride + 2 * ch
                grown = jnp.concatenate(
                    [
                        jnp.broadcast_to(wide_taps[at + o : at + o + 1], (SUB, reach))
                        for o in range(bands)
                    ],
                    0,
                )
                total = jnp.where(step_out == a, grown, total)
            out.append(total)
        return jnp.concatenate(out, 0).astype(BF)

    t_first = conv_taps(0)
    t_second = conv_taps(ch)
    t_output = output_taps()

    tall_up = ups.shape[1]
    ups[0] = ext[0][SUB - 3 : SUB - 3 + tall_up, :]
    for level in range(1, n):
        rows, cols = shapes[level]
        e = ext[level]
        scale = 2.0 ** -level
        shape = (tall_up, e.shape[0])
        where_to = ((iota(shape, 0) - 3).astype(F32) + 0.5) * scale - 0.5
        along = jnp.maximum(
            0.0, 1.0 - jnp.abs(where_to - (iota(shape, 1) - SUB).astype(F32))
        ).astype(BF)
        hi, mid, lo = [dot(along, p) for p in parts(e[...], 3)]
        grown = hi + (mid + lo)
        shape = (e.shape[1], wide)
        pixel = iota(shape, 1)
        pixel = jnp.where(pixel < cols_dev + LANES // 2, pixel, pixel - wide)
        cell = iota(shape, 0)
        cell = jnp.where(cell < (cols + e.shape[1]) // 2, cell, cell - e.shape[1])
        where_to = (pixel.astype(F32) + 0.5) * scale - 0.5
        along = jnp.maximum(0.0, 1.0 - jnp.abs(where_to - cell.astype(F32))).astype(BF)
        hi, mid, lo = [dot(p, along) for p in parts(grown, 3)]
        ups[level] = hi + (mid + lo)

    def inside(field, start, margin):
        index = iota(field.shape, 0)
        begin = margin - start - lat * rows_dev
        keep = (index >= begin * ch) & (index < (begin + rows_dev * lats) * ch)
        return jnp.where(keep, field, 0.0)

    def mix_step(g, carry):
        here = pl.ds(pl.multiple_of(g * SUB, SUB), SUB)
        x = jnp.concatenate([ups[level, here, :] for level in range(n)], 0).astype(BF)
        f = jnp.maximum(dot(t_levels, x), 0.0).astype(BF)
        s = jnp.maximum(dot(t_hidden, f), 0.0)
        second[pl.ds(pl.multiple_of(g * deep, deep), deep), :] = inside(s, g * SUB, 3).astype(BF)
        return carry

    lax.fori_loop(0, tall_up // SUB, mix_step, 0)

    def conv_pass(src, dst, weights, count, margin):
        def step_fn(k, carry):
            start = jnp.minimum(k * SUB, count - SUB)
            at = pl.multiple_of(start * ch, 2 * ch)
            x = src[pl.ds(at, reach), :]
            p = dot(weights, x)
            c = (
                p[deep : 2 * deep]
                + pltpu.roll(p[:deep], 1, 1)
                + pltpu.roll(p[2 * deep :], wide - 1, 1)
            )
            r = x.astype(F32)[ch : ch + deep] + jnp.maximum(c, 0.0)
            dst[pl.ds(at, deep), :] = inside(r, start, margin).astype(BF)
            return carry

        lax.fori_loop(0, (count + SUB - 1) // SUB, step_fn, 0)

    conv_pass(second, third, t_first, rows_dev + 4, 2)
    conv_pass(third, fourth, t_second, rows_dev + 2, 1)

    def output_step(k, carry):
        squares, grad = carry
        x = fourth[pl.ds(pl.multiple_of(k * deep, deep), reach), :]
        p = dot(t_output, x)
        m = bands * SUB
        c = p[m : 2 * m] + pltpu.roll(p[:m], 1, 1) + pltpu.roll(p[2 * m :], wide - 1, 1)
        c = c[:, :cols_dev]
        here = pl.ds(pl.multiple_of(k * SUB, SUB), SUB)
        for o in range(bands):
            recon[o, here, :] = c[o * SUB : (o + 1) * SUB]
        error = c - jnp.concatenate([target[o, here, :] for o in range(bands)], 0)
        slope = (2.0 * error / pixel_count).astype(BF).astype(F32)
        slope = jnp.concatenate([slope, jnp.zeros((m, wide - cols_dev), F32)], 1)
        slopes = jnp.concatenate(
            [pltpu.roll(slope, wide - 1, 1), slope, pltpu.roll(slope, 1, 1)], 0
        ).astype(BF)
        grad = grad + lax.dot_general(
            slopes, x, (((1,), (1,)), ((), ())), preferred_element_type=F32
        )
        return squares + error * error, grad

    m = bands * SUB
    squares, grad = lax.fori_loop(
        0,
        rows_dev // SUB,
        output_step,
        (jnp.zeros((m, cols_dev), F32), jnp.zeros((3 * m, reach), F32)),
    )
    pad = -reach % LANES
    grad = jnp.concatenate([grad, jnp.zeros((3 * m, pad), F32)], 1)
    line = iota(grad.shape, 0) & 7
    aligned = grad
    for y in range(1, SUB):
        aligned = jnp.where(line == y, pltpu.roll(grad, reach + pad - y * ch, 1), aligned)
    folded = jnp.sum(aligned[:, :LANES].reshape(3 * bands, SUB, LANES), axis=1)
    sums = jnp.concatenate([folded, jnp.zeros((part.shape[0] - 3 * bands, LANES), F32)], 0)

    shape = part.shape
    last = iota(shape, 0) == 3 * bands

    def put(sums, lane, value):
        return jnp.where(last & (iota(shape, 1) == lane), value, sums)

    sums = put(sums, 0, jnp.sum(squares))

    for level, (rows, cols) in enumerate(shapes):
        e = ext[level]
        cover = max(cols, LANES)
        full = e.shape[1]
        scale = anchor[level]
        odd = lat * rows + lon * cols + parity[level]

        def rate_step(g, total, level=level, rows=rows, cols=cols, e=e, cover=cover, full=full, scale=scale, odd=odd):
            window = e[pl.ds(pl.multiple_of(g * SUB, SUB), 3 * SUB), :]
            moved = {i: window[SUB + i : 2 * SUB + i] for i in range(-2, 3)}
            context = [
                (moved[i] if j == 0 else pltpu.roll(moved[i], (-j) % full, 1))[:, :cover]
                for i, j in context_steps
            ]
            inner = jnp.maximum(dot_pairs(a_in, jnp.concatenate(context, 0)), 0.0)
            outer = jnp.maximum(dot_pairs(a_mid, inner), 0.0)
            raw = dot_pairs(a_out, outer)
            mu, sigma = raw[:SUB], raw[SUB:]
            row, col = iota((SUB, cover), 0), iota((SUB, cover), 1)
            first = ((row + col + odd) & 1) == 0
            centre = jnp.where(first, 0.0, mu)
            soft = jnp.maximum(sigma, 0.0) + jnp.log1p(jnp.exp(-jnp.abs(sigma)))
            spread = jnp.where(first, scale, 0.1 + soft)
            bits = laplace_bits(moved[0][:, :cover] - centre, spread)
            if level == 0:
                bits_out[pl.ds(pl.multiple_of(g * SUB, SUB), SUB), :] = bits
            if rows < SUB or cols < LANES:
                bits = jnp.where((row < rows) & (col < cols), bits, 0.0)
            return total + bits

        total = lax.fori_loop(0, max(1, rows // SUB), rate_step, jnp.zeros((SUB, cover), F32))
        sums = put(sums, 1 + level, jnp.sum(total))
    part[...] = sums


def local(target, *args):
    latents = args[:-11]
    (
        tile_seeds, anchor_parity, anchor_scale, mix_levels, mix_hidden,
        conv_first, conv_second, conv_output, context_in, context_mid, context_out,
    ) = args[-11:]
    n = len(latents)
    shapes = [x.shape for x in latents]
    bands, rows_dev, cols_dev = target.shape
    ch = mix_hidden.shape[0]
    devices = lax.axis_size("lat") * lax.axis_size("lon")
    pixel_count = float(bands * rows_dev * cols_dev * devices)
    vmem = pl.BlockSpec(memory_space=pltpu.VMEM)
    smem = pl.BlockSpec(memory_space=pltpu.SMEM)
    wides = [width_of(c) for _, c in shapes]
    talls = [max(r, SUB) for r, _ in shapes]
    edge = pltpu.VMEM((sum(talls), LANES), F32)
    belt = pltpu.VMEM((SUB, sum(wides)), F32)
    extended = pl.pallas_call(
        functools.partial(halo_kernel, shapes),
        out_shape=[
            jax.ShapeDtypeStruct((t + 2 * SUB, w), F32) for t, w in zip(talls, wides)
        ],
        in_specs=[smem] + [vmem] * n,
        out_specs=[vmem] * n,
        scratch_shapes=[edge] * 4
        + [belt] * 4
        + [pltpu.SemaphoreType.DMA((4,)), pltpu.SemaphoreType.DMA((4,))],
        compiler_params=pltpu.CompilerParams(
            collective_id=0, has_side_effects=True, vmem_limit_bytes=16 * 2**20
        ),
        name="halo",
    )(tile_seeds, *latents)
    taps = jnp.concatenate([conv_first, conv_second, conv_output], 0).transpose(2, 3, 0, 1)
    taps = jnp.pad(taps, ((0, 0), (0, 0), (0, -taps.shape[2] % SUB), (0, 0))).reshape(-1, ch)
    wide = wides[0]
    tall_up = rows_dev + SUB
    recon, bits, part = pl.pallas_call(
        functools.partial(local_kernel, shapes, ch, bands, pixel_count),
        out_shape=[
            jax.ShapeDtypeStruct(target.shape, F32),
            jax.ShapeDtypeStruct((rows_dev, cols_dev), F32),
            jax.ShapeDtypeStruct((2 * SUB, LANES), F32),
        ],
        in_specs=[vmem] * (n + 1) + [smem] * 2 + [vmem] * 6,
        out_specs=[vmem] * 3,
        scratch_shapes=[
            pltpu.VMEM((n, tall_up, wide), F32),
            pltpu.VMEM((tall_up * ch, wide), BF),
            pltpu.VMEM(((rows_dev + 4) * ch, wide), BF),
            pltpu.VMEM(((rows_dev + 2) * ch, wide), BF),
        ],
        compiler_params=pltpu.CompilerParams(vmem_limit_bytes=48 * 2**20),
        name="step",
    )(
        *extended, target, anchor_parity, anchor_scale, mix_levels, mix_hidden,
        taps, context_in, context_mid, context_out,
    )
    total = lax.psum(part, ("lat", "lon"))
    grad = total[: 3 * bands, : 3 * ch].reshape(3, bands, 3, ch).transpose(1, 3, 2, 0)
    counts = jnp.array(
        [pixel_count] + [float(r * c * devices) for r, c in shapes], dtype=F32
    )
    loss_terms = total[3 * bands, : n + 1] / counts
    return (recon, bits, loss_terms, grad)


def solution(mesh):
    both = P("lat", "lon")
    return jax.shard_map(
        local,
        mesh=mesh,
        in_specs=(P(None, "lat", "lon"),) + (both,) * 7 + (P(),) * 10,
        out_specs=(P(None, "lat", "lon"), both, P(), P()),
        check_vma=False,
    )
```

time: 535 us -> 95.5 us (0.18); the launches traced: 525 us -> 95.1 us
  matrix products: 246 us -> 0 us
  local copies, waits for them, and re-layouts: 142 us -> 5.65 us
  starting transfers between devices: 57.9 us -> 0 us
  Pallas kernels: 0 us -> 49 us
  other arithmetic: 34.9 us -> 0.62 us
    conv_general_dilated x3 -> x0, matrix products: 224 us -> none  [conv_valid(): lax.conv_general_dilated(field[None], kernel, (1, 1), ((0, 0), (0, 0)), d...]
    ppermute x24 -> x0, starting transfers between devices: 57.9 us -> none  [the longest x12 29 us: padded_2(): before = lax.ppermute(last, axis, up)]
    conv_general_dilated x11 -> x0, local copies, waits for them, and re-layouts: 54.5 us -> none  [conv_valid(): lax.conv_general_dilated(field[None], kernel, (1, 1), ((0, 0), (0, 0)), d...]
    pallas_call x0 -> x2, Pallas kernels: none -> 49 us  [the longest x1 36.4 us: local(): pl.pallas_call(functools.partial(local_kernel, shapes, ch, bands, pixel_c...]
    max x4 -> x0, local copies, waits for them, and re-layouts: 42.3 us -> none  [the longest x2 21.4 us: local(): jax.nn.relu(conv_valid(deeper, conv_first))]
    another operation x56 -> x0, local copies, waits for them, and re-layouts: 24.8 us -> none  [the longest x48 14.7 us: level_bits(): jnp.stack([extended[2 + row_step:2 + row_step + rows_in, 2 + col_step:2 +...]
    dot_general x28 -> x0, matrix products: 21.9 us -> none  [the longest x9 7.43 us: local(): jnp.einsum('ohw,chw->oc', slope, window, preferred_element_type=jnp.float32)]
    reduce_sum x7 -> x0, other arithmetic: 14.9 us -> none  [the longest x6 13 us: local(): bit_sums.append(jnp.sum(bits))]
  transfers between devices with their start and end apart: 24 -> 0, of which waited for: 0 -> 0; matrix products, arithmetic and copies ran while one was open for 8% -> 0% of each run, Pallas kernels for 0% -> 0%
where the time goes in v1:
time: 95.5 us; the launch traced here: 95.1 us
  Pallas kernels  49 us (51%)
  blocking collectives  38.4 us (40%)
  local copies, waits for them, and re-layouts  5.65 us (6%)
  between operations  1.48 us (2%)
    psum x1, blocking collectives, local(): total = lax.psum(part, ('lat', 'lon'))  38.4 us
    pallas_call x1, Pallas kernels, local(): pl.pallas_call(functools.partial(local_kernel, shapes, ch, bands, pixel_c...  36.4 us
    pallas_call x1, Pallas kernels, local(): pl.pallas_call(functools.partial(halo_kernel, shapes), out_shape=[jax.Sha...  12.6 us
    unnamed x38, local copies, waits for them, and re-layouts  4.93 us

profile of v1, /device:TPU:0, one launch (start us, length us, event | category | flops | bytes accessed | tf_op | source)
XLA Modules:
  0.0 95.1 jit_solution(14408372103477765630)
XLA Ops:
  1.3 0.8 copy.31.refs_9_
  2.1 0.1 copy.32.refs_12_
  2.2 0.9 copy.27
  3.1 0.0 copy-start.13
  3.1 0.1 copy.28
  3.2 0.6 copy-done.13
  3.8 0.1 copy.29
  3.9 0.1 maximum_bitcast_fusion
  4.1 0.2 copy.34
  4.2 0.0 copy-start.4
  4.2 0.0 copy-start.6
  4.3 0.0 copy-start.8
  4.3 0.8 copy-done.1
  5.1 0.0 copy-start.3
  5.2 12.6 %halo.1 = (f32[80,640]{1,0:T(8,128)S(1)}, f32[48,384]{1,0:T(8,128)S(1)}, f32[32,256]{1,0:T(8,128)S(1)}, f32[24,128]{1,0:T(8,128)S(1)}, f32[24,128]{1,0:T(8,128)S(1)}, /*index=5*/f32[24,128]{1,0:T(8,128)S(1)}) custom-call(s32[1,1]{1,0:T(1,128)S(6)} %copy.37.seed_ref, f32[64,512]{1,0:T(8,128)S(1)} %copy-done.1, f32[32,256]{1,0:T(8,128)S(1)} %copy-done.2, ...), custom_call_target="tpu_custom_call" | custom-call | tf_op jit(solution)/shard_map/halo/pallas_call | solution.py:423
  17.8 0.0 copy-start.5
  17.8 0.0 copy-start.9
  17.8 0.6 copy-done.5
  18.5 36.4 %step.1 = (f32[3,64,512]{2,1,0:T(8,128)}, f32[64,512]{1,0:T(8,128)}, f32[16,128]{1,0:T(8,128)S(1)}) custom-call(f32[80,640]{1,0:T(8,128)S(1)} %get-tuple-element.13.refs_0_, f32[48,384]{1,0:T(8,128)S(1)} %get-tuple-element.14.refs_1_, f32[32,256]{1,0:T(8,128)S(1)} %get-tuple-element.15.refs_2_, f32[24,128]{1,0:T(8,128)S(1)} %get-tuple-element.16.refs_3_, ...), custom_call_target="tpu_custom_call" | custom-call | tf_op jit(solution)/shard_map/step/pallas_call | solution.py:442
  54.9 38.4 %psum.7 = f32[16,128]{1,0:T(8,128)S(1)} all-reduce(f32[16,128]{1,0:T(8,128)S(1)} %get-tuple-element.21), channel_id=1, replica_groups=mesh['lat'=4,'lon'=8] {'lat','lon'}, use_global_device_ids=true, to_apply=%region_0.1 | all-reduce | flops 2048 | bytes 16384 | tf_op jit(solution)/shard_map/psum | solution.py:463
  93.2 0.7 copy-done.15
  93.9 0.5 fusion
  94.4 0.1 reshape.15
  94.5 0.6 copy.36
  (22 shorter events, 0.1 us)
Async XLA Ops:
  0.6 1.4 %copy-start.14 = (f32[24,12]{0,1:T(8,128)S(1)}, f32[24,12]{0,1:T(8,128)}, u32[]{:S(2)}) copy-start(f32[24,12]{0,1:T(8,128)} %param.34) | copy-start | bytes 3460
  2.2 0.9 copy-start.12
  3.1 0.7 copy-start.13
  3.9 13.9 %copy-start = (f32[3,64,512]{2,1,0:T(8,128)S(1)}, f32[3,64,512]{2,1,0:T(8,128)}, u32[]{:S(2)}) copy-start(f32[3,64,512]{2,1,0:T(8,128)} %refs_6_.1) | copy-start | bytes 1179652
  4.2 0.9 copy-start.1
  4.2 0.9 copy-start.2
  4.2 0.9 copy-start.4
  4.2 0.9 copy-start.6
  4.3 0.9 copy-start.7
  4.3 0.8 copy-start.8
  5.1 12.7 %copy-start.3 = (f32[24,24]{1,0:T(8,128)S(1)}, f32[24,24]{1,0:T(8,128)}, u32[]{:S(2)}) copy-start(f32[24,24]{1,0:T(8,128)} %refs_13_.1) | copy-start | bytes 6916
  5.2 12.7 %copy-start.11 = (f32[6]{0:T(128)S(1)}, f32[6]{0:T(128)}, u32[]{:S(2)}) copy-start(f32[6]{0:T(128)} %refs_8_.1) | copy-start | bytes 76
  17.8 0.7 copy-start.5
  17.8 0.7 copy-start.9
  17.8 0.7 copy-start.10
  93.2 0.7 copy-start.15

commit v2 on v1

--- a/solution.py
+++ b/solution.py
@@ -140,6 +140,52 @@
         lane0 += wide
 
 
+def sum_kernel(part, total, row, col, send_sem, recv_sem):
+    place = {"lon": lax.axis_index("lon"), "lat": lax.axis_index("lat")}
+    barrier = pltpu.get_barrier_semaphore()
+
+    def peers(axis):
+        size = lax.axis_size(axis)
+        for d in range(1, size):
+            yield d - 1, {**place, axis: lax.rem(place[axis] + d, size)}
+
+    count = 0
+    for axis in ("lon", "lat"):
+        for _, other in peers(axis):
+            pl.semaphore_signal(
+                barrier, inc=1, device_id=(other["lat"], other["lon"]), device_id_type=MESH
+            )
+            count += 1
+    row[place["lon"]] = part[...]
+    pl.semaphore_wait(barrier, count)
+    first = 0
+    for axis, slots in (("lon", row), ("lat", col)):
+        mine = slots.at[place[axis]]
+        copies = [
+            pltpu.make_async_remote_copy(
+                src_ref=mine,
+                dst_ref=mine,
+                send_sem=send_sem.at[first + d],
+                recv_sem=recv_sem.at[first + d],
+                device_id=(other["lat"], other["lon"]),
+                device_id_type=MESH,
+            )
+            for d, other in peers(axis)
+        ]
+        for copy in copies:
+            copy.start()
+        for copy in copies:
+            copy.wait()
+        first += len(copies)
+        added = slots[0]
+        for d in range(1, lax.axis_size(axis)):
+            added = added + slots[d]
+        if axis == "lon":
+            col[place["lat"]] = added
+        else:
+            total[...] = added
+
+
 def dot(a, b):
     return jnp.dot(a, b, preferred_element_type=F32)
 
@@ -160,6 +206,23 @@
 
 def div_24(x):
     return (x * 2731) >> 16
+
+
+def looped(count, most, body, carry):
+    each = next(k for k in range(min(most, count), 0, -1) if count % k == 0)
+
+    def turn(t, carry):
+        for k in range(each):
+            carry = body(t * each + k, carry)
+        return carry
+
+    if each == count:
+        return turn(0, carry)
+    return lax.fori_loop(0, count // each, turn, carry)
+
+
+def aligned(value, by):
+    return value if isinstance(value, int) else pl.multiple_of(value, by)
 
 
 def one_hot(flag):
@@ -293,19 +356,19 @@
         return jnp.where(keep, field, 0.0)
 
     def mix_step(g, carry):
-        here = pl.ds(pl.multiple_of(g * SUB, SUB), SUB)
+        here = pl.ds(aligned(g * SUB, SUB), SUB)
         x = jnp.concatenate([ups[level, here, :] for level in range(n)], 0).astype(BF)
         f = jnp.maximum(dot(t_levels, x), 0.0).astype(BF)
         s = jnp.maximum(dot(t_hidden, f), 0.0)
-        second[pl.ds(pl.multiple_of(g * deep, deep), deep), :] = inside(s, g * SUB, 3).astype(BF)
+        second[pl.ds(aligned(g * deep, deep), deep), :] = inside(s, g * SUB, 3).astype(BF)
         return carry
 
-    lax.fori_loop(0, tall_up // SUB, mix_step, 0)
+    looped(tall_up // SUB, 3, mix_step, 0)
 
     def conv_pass(src, dst, weights, count, margin):
         def step_fn(k, carry):
-            start = jnp.minimum(k * SUB, count - SUB)
-            at = pl.multiple_of(start * ch, 2 * ch)
+            start = min(k * SUB, count - SUB) if isinstance(k, int) else jnp.minimum(k * SUB, count - SUB)
+            at = aligned(start * ch, 2 * ch)
             x = src[pl.ds(at, reach), :]
             p = dot(weights, x)
             c = (
@@ -317,19 +380,19 @@
             dst[pl.ds(at, deep), :] = inside(r, start, margin).astype(BF)
             return carry
 
-        lax.fori_loop(0, (count + SUB - 1) // SUB, step_fn, 0)
+        looped((count + SUB - 1) // SUB, 3, step_fn, 0)
 
     conv_pass(second, third, t_first, rows_dev + 4, 2)
     conv_pass(third, fourth, t_second, rows_dev + 2, 1)
 
     def output_step(k, carry):
         squares, grad = carry
-        x = fourth[pl.ds(pl.multiple_of(k * deep, deep), reach), :]
+        x = fourth[pl.ds(aligned(k * deep, deep), reach), :]
         p = dot(t_output, x)
         m = bands * SUB
         c = p[m : 2 * m] + pltpu.roll(p[:m], 1, 1) + pltpu.roll(p[2 * m :], wide - 1, 1)
         c = c[:, :cols_dev]
-        here = pl.ds(pl.multiple_of(k * SUB, SUB), SUB)
+        here = pl.ds(aligned(k * SUB, SUB), SUB)
         for o in range(bands):
             recon[o, here, :] = c[o * SUB : (o + 1) * SUB]
         error = c - jnp.concatenate([target[o, here, :] for o in range(bands)], 0)
@@ -344,19 +407,19 @@
         return squares + error * error, grad
 
     m = bands * SUB
-    squares, grad = lax.fori_loop(
-        0,
+    squares, grad = looped(
         rows_dev // SUB,
+        4,
         output_step,
         (jnp.zeros((m, cols_dev), F32), jnp.zeros((3 * m, reach), F32)),
     )
     pad = -reach % LANES
     grad = jnp.concatenate([grad, jnp.zeros((3 * m, pad), F32)], 1)
     line = iota(grad.shape, 0) & 7
-    aligned = grad
+    moved = grad
     for y in range(1, SUB):
-        aligned = jnp.where(line == y, pltpu.roll(grad, reach + pad - y * ch, 1), aligned)
-    folded = jnp.sum(aligned[:, :LANES].reshape(3 * bands, SUB, LANES), axis=1)
+        moved = jnp.where(line == y, pltpu.roll(grad, reach + pad - y * ch, 1), moved)
+    folded = jnp.sum(moved[:, :LANES].reshape(3 * bands, SUB, LANES), axis=1)
     sums = jnp.concatenate([folded, jnp.zeros((part.shape[0] - 3 * bands, LANES), F32)], 0)
 
     shape = part.shape
@@ -375,7 +438,7 @@
         odd = lat * rows + lon * cols + parity[level]
 
         def rate_step(g, total, level=level, rows=rows, cols=cols, e=e, cover=cover, full=full, scale=scale, odd=odd):
-            window = e[pl.ds(pl.multiple_of(g * SUB, SUB), 3 * SUB), :]
+            window = e[pl.ds(aligned(g * SUB, SUB), 3 * SUB), :]
             moved = {i: window[SUB + i : 2 * SUB + i] for i in range(-2, 3)}
             context = [
                 (moved[i] if j == 0 else pltpu.roll(moved[i], (-j) % full, 1))[:, :cover]
@@ -392,12 +455,12 @@
             spread = jnp.where(first, scale, 0.1 + soft)
             bits = laplace_bits(moved[0][:, :cover] - centre, spread)
             if level == 0:
-                bits_out[pl.ds(pl.multiple_of(g * SUB, SUB), SUB), :] = bits
+                bits_out[pl.ds(aligned(g * SUB, SUB), SUB), :] = bits
             if rows < SUB or cols < LANES:
                 bits = jnp.where((row < rows) & (col < cols), bits, 0.0)
             return total + bits
 
-        total = lax.fori_loop(0, max(1, rows // SUB), rate_step, jnp.zeros((SUB, cover), F32))
+        total = looped(max(1, rows // SUB), 4, rate_step, jnp.zeros((SUB, cover), F32))
         sums = put(sums, 1 + level, jnp.sum(total))
     part[...] = sums
 
@@ -460,7 +523,23 @@
         *extended, target, anchor_parity, anchor_scale, mix_levels, mix_hidden,
         taps, context_in, context_mid, context_out,
     )
-    total = lax.psum(part, ("lat", "lon"))
+    lats, lons = lax.axis_size("lat"), lax.axis_size("lon")
+    total = pl.pallas_call(
+        sum_kernel,
+        out_shape=jax.ShapeDtypeStruct(part.shape, F32),
+        in_specs=[vmem],
+        out_specs=vmem,
+        scratch_shapes=[
+            pltpu.VMEM((lons,) + part.shape, F32),
+            pltpu.VMEM((lats,) + part.shape, F32),
+            pltpu.SemaphoreType.DMA((lats + lons - 2,)),
+            pltpu.SemaphoreType.DMA((lats + lons - 2,)),
+        ],
+        compiler_params=pltpu.CompilerParams(
+            collective_id=1, has_side_effects=True, vmem_limit_bytes=8 * 2**20
+        ),
+        name="sums",
+    )(part)
     grad = total[: 3 * bands, : 3 * ch].reshape(3, bands, 3, ch).transpose(1, 3, 2, 0)
     counts = jnp.array(
         [pixel_count] + [float(r * c * devices) for r, c in shapes], dtype=F32

time: 95.5 us -> 56.8 us (0.59)
  blocking collectives: 38.4 us -> 0 us
    psum x1 -> x0, blocking collectives: 38.4 us -> none  [local(): total = lax.psum(part, ('lat', 'lon'))]
    pallas_call x1, Pallas kernels: 36.4 us -> 27.4 us  [local(): pl.pallas_call(functools.partial(local_kernel, shapes, ch, bands, pixel_c...]
    pallas_call x0 -> x1, Pallas kernels: none -> 8.69 us  [local(): pl.pallas_call(sum_kernel, out_shape=jax.ShapeDtypeStruct(part.shape, F32...]
where the time goes in v2:
time: 56.8 us; the launch traced here: 56.5 us
  Pallas kernels  48.7 us (86%)
  local copies, waits for them, and re-layouts  5.64 us (10%)
  between operations  1.49 us (3%)
  other arithmetic  0.62 us (1%)
    pallas_call x1, Pallas kernels, local(): pl.pallas_call(functools.partial(local_kernel, shapes, ch, bands, pixel_c...  27.4 us
    pallas_call x1, Pallas kernels, local(): pl.pallas_call(functools.partial(halo_kernel, shapes), out_shape=[jax.Sha...  12.6 us
    pallas_call x1, Pallas kernels, local(): pl.pallas_call(sum_kernel, out_shape=jax.ShapeDtypeStruct(part.shape, F32...  8.69 us
    unnamed x38, local copies, waits for them, and re-layouts  4.92 us

profile of v2, /device:TPU:0, one launch (start us, length us, event | category | flops | bytes accessed | tf_op | source)
XLA Modules:
  0.0 56.5 jit_solution(15979032060022266197)
XLA Ops:
  1.3 0.8 %copy.31.refs_9_ = bf16[24,6]{1,0:T(8,128)(2,1)S(1)} copy(bf16[24,6]{0,1:T(8,128)(2,1)} %param.29) | data formatting | bytes 576 | tf_op args[10]
  2.1 0.1 copy.32.refs_12_
  2.2 0.9 %copy.27 = bf16[24,24,3,3]{0,1,3,2:T(8,128)(2,1)S(1)} copy(bf16[24,24,3,3]{1,0,3,2:T(8,128)(2,1)} %param.31) | data formatting | bytes 20736 | tf_op args[12]
  3.1 0.0 copy-start.13
  3.1 0.1 copy.28
  3.2 0.6 %copy-done.13 = bf16[3,24,3,3]{1,3,2,0:T(4,128)(2,1)S(1)} copy-done((bf16[3,24,3,3]{1,3,2,0:T(4,128)(2,1)S(1)}, bf16[3,24,3,3]{1,3,2,0:T(4,128)(2,1)}, u32[]{:S(2)}) %copy-start.13) | copy-done | bytes 1320
  3.8 0.1 copy.29
  3.9 0.1 maximum_bitcast_fusion
  4.1 0.2 copy.34
  4.2 0.0 copy-start.4
  4.2 0.0 copy-start.6
  4.3 0.0 copy-start.8
  4.3 0.8 %copy-done.1 = f32[64,512]{1,0:T(8,128)S(1)} copy-done((f32[64,512]{1,0:T(8,128)S(1)}, f32[64,512]{1,0:T(8,128)}, u32[]{:S(2)}) %copy-start.1) | copy-done | bytes 131096
  5.2 12.6 %halo.1 = (f32[80,640]{1,0:T(8,128)S(1)}, f32[48,384]{1,0:T(8,128)S(1)}, f32[32,256]{1,0:T(8,128)S(1)}, f32[24,128]{1,0:T(8,128)S(1)}, f32[24,128]{1,0:T(8,128)S(1)}, /*index=5*/f32[24,128]{1,0:T(8,128)S(1)}) custom-call(s32[1,1]{1,0:T(1,128)S(6)} %copy.37.seed_ref, f32[64,512]{1,0:T(8,128)S(1)} %copy-done.1, f32[32,256]{1,0:T(8,128)S(1)} %copy-done.2, ...), custom_call_target="tpu_custom_call" | custom-call | tf_op jit(solution)/shard_map/halo/pallas_call | solution.py:486
  17.8 0.0 copy-start.5
  17.8 0.0 copy-start.9
  17.8 0.6 %copy-done.5 = bf16[24,24]{1,0:T(8,128)(2,1)S(1)} copy-done((bf16[24,24]{1,0:T(8,128)(2,1)S(1)}, bf16[24,24]{1,0:T(8,128)(2,1)}, u32[]{:S(2)}) %copy-start.5) | copy-done | bytes 1176
  18.5 27.4 %step.1 = (f32[3,64,512]{2,1,0:T(8,128)}, f32[64,512]{1,0:T(8,128)}, f32[16,128]{1,0:T(8,128)S(1)}) custom-call(f32[80,640]{1,0:T(8,128)S(1)} %get-tuple-element.13.refs_0_, f32[48,384]{1,0:T(8,128)S(1)} %get-tuple-element.14.refs_1_, f32[32,256]{1,0:T(8,128)S(1)} %get-tuple-element.15.refs_2_, f32[24,128]{1,0:T(8,128)S(1)} %get-tuple-element.16.refs_3_, ...), custom_call_target="tpu_custom_call" | custom-call | tf_op jit(solution)/shard_map/step/pallas_call | solution.py:505
  45.9 8.7 %sums.1 = f32[16,128]{1,0:T(8,128)S(1)} custom-call(f32[16,128]{1,0:T(8,128)S(1)} %get-tuple-element.21.part), custom_call_target="tpu_custom_call" | custom-call | tf_op jit(solution)/shard_map/sums/pallas_call | solution.py:527
  54.6 0.0 copy-start.15
  54.6 0.6 %copy-done.15 = f32[1,7]{1,0:T(1,128)S(1)} copy-done((f32[1,7]{1,0:T(1,128)S(1)}, f32[1,7]{1,0:T(1,128)}, u32[]{:S(2)}) %copy-start.15) | copy-done | bytes 52
  55.3 0.5 multiply_bitcast_fusion
  55.8 0.1 reshape.15
  55.9 0.6 %copy.36 = f32[3,3,3,24]{3,0,2,1:T(4,128)} copy(f32[3,3,3,24]{3,2,1,0:T(4,128)S(1)} %reshape.15) | data formatting | bytes 5184 | tf_op jit(solution)/shard_map/reshape | solution.py:543
  (22 shorter events, 0.1 us)
Async XLA Ops:
  0.6 1.4 %copy-start.14 = (f32[24,12]{0,1:T(8,128)S(1)}, f32[24,12]{0,1:T(8,128)}, u32[]{:S(2)}) copy-start(f32[24,12]{0,1:T(8,128)} %param.34) | copy-start | bytes 3460
  2.2 0.9 %copy-start.12 = (bf16[24,24,3,3]{1,0,3,2:T(8,128)(2,1)S(1)}, bf16[24,24,3,3]{1,0,3,2:T(8,128)(2,1)}, u32[]{:S(2)}) copy-start(bf16[24,24,3,3]{1,0,3,2:T(8,128)(2,1)} %param.32) | copy-start | bytes 31108
  3.1 0.7 %copy-start.13 = (bf16[3,24,3,3]{1,3,2,0:T(4,128)(2,1)S(1)}, bf16[3,24,3,3]{1,3,2,0:T(4,128)(2,1)}, u32[]{:S(2)}) copy-start(bf16[3,24,3,3]{1,3,2,0:T(4,128)(2,1)} %param.33) | copy-start | bytes 3892
  3.9 13.9 %copy-start = (f32[3,64,512]{2,1,0:T(8,128)S(1)}, f32[3,64,512]{2,1,0:T(8,128)}, u32[]{:S(2)}) copy-start(f32[3,64,512]{2,1,0:T(8,128)} %refs_6_.1) | copy-start | bytes 1179652
  4.2 0.9 %copy-start.1 = (f32[64,512]{1,0:T(8,128)S(1)}, f32[64,512]{1,0:T(8,128)}, u32[]{:S(2)}) copy-start(f32[64,512]{1,0:T(8,128)} %refs_0_.1) | copy-start | bytes 393220
  4.2 0.9 %copy-start.2 = (f32[32,256]{1,0:T(8,128)S(1)}, f32[32,256]{1,0:T(8,128)}, u32[]{:S(2)}) copy-start(f32[32,256]{1,0:T(8,128)} %refs_1_.1) | copy-start | bytes 98308
  4.2 0.9 %copy-start.4 = (f32[16,128]{1,0:T(8,128)S(1)}, f32[16,128]{1,0:T(8,128)}, u32[]{:S(2)}) copy-start(f32[16,128]{1,0:T(8,128)} %refs_2_.1) | copy-start | bytes 24580
  4.2 0.9 %copy-start.6 = (f32[8,64]{1,0:T(8,128)S(1)}, f32[8,64]{1,0:T(8,128)}, u32[]{:S(2)}) copy-start(f32[8,64]{1,0:T(8,128)} %refs_3_.1) | copy-start | bytes 6148
  4.3 0.9 %copy-start.7 = (f32[4,32]{1,0:T(4,128)S(1)}, f32[4,32]{1,0:T(4,128)}, u32[]{:S(2)}) copy-start(f32[4,32]{1,0:T(4,128)} %refs_4_.1) | copy-start | bytes 1540
  4.3 0.8 %copy-start.8 = (f32[2,16]{1,0:T(2,128)S(1)}, f32[2,16]{1,0:T(2,128)}, u32[]{:S(2)}) copy-start(f32[2,16]{1,0:T(2,128)} %refs_5_.1) | copy-start | bytes 388
  5.1 12.7 %copy-start.3 = (f32[24,24]{1,0:T(8,128)S(1)}, f32[24,24]{1,0:T(8,128)}, u32[]{:S(2)}) copy-start(f32[24,24]{1,0:T(8,128)} %refs_13_.1) | copy-start | bytes 6916
  5.2 12.7 %copy-start.11 = (f32[6]{0:T(128)S(1)}, f32[6]{0:T(128)}, u32[]{:S(2)}) copy-start(f32[6]{0:T(128)} %refs_8_.1) | copy-start | bytes 76
  17.8 0.7 %copy-start.5 = (bf16[24,24]{1,0:T(8,128)(2,1)S(1)}, bf16[24,24]{1,0:T(8,128)(2,1)}, u32[]{:S(2)}) copy-start(bf16[24,24]{1,0:T(8,128)(2,1)} %refs_10_.1) | copy-start | bytes 3460
  17.8 0.7 %copy-start.9 = (f32[2,24]{1,0:T(2,128)S(1)}, f32[2,24]{1,0:T(2,128)}, u32[]{:S(2)}) copy-start(f32[2,24]{1,0:T(2,128)} %refs_14_.1) | copy-start | bytes 580
  17.8 0.7 %copy-start.10 = (s32[6]{0:T(128)S(1)}, s32[6]{0:T(128)}, u32[]{:S(2)}) copy-start(s32[6]{0:T(128)} %refs_7_.1) | copy-start | bytes 76
  54.6 0.7 %copy-start.15 = (f32[1,7]{1,0:T(1,128)S(1)}, f32[1,7]{1,0:T(1,128)}, u32[]{:S(2)}) copy-start(f32[1,7]{1,0:T(1,128)} %constant.11) | copy-start | bytes 88

commit v3 on v2

--- a/solution.py
+++ b/solution.py
@@ -201,7 +201,12 @@
 
 def dot_pairs(a, x):
     hi, lo = parts(x, 2)
-    return dot(a[0], hi) + (dot(a[1], hi) + dot(a[0], lo))
+    m, k = a.shape[0] // 2, a.shape[1]
+    if k == 2 * x.shape[0]:
+        p = dot(a, jnp.concatenate([hi, lo], 0))
+        return p[:m] + p[m:]
+    p = dot(a, hi)
+    return p[:m] + (p[m:] + dot(a[:m], lo))
 
 
 def div_24(x):
@@ -247,7 +252,7 @@
     n = len(shapes)
     ext = refs[:n]
     (
-        target, parity, anchor, mix_l, mix_h, taps, c_in, c_mid, c_out,
+        target, parity, anchor, mix_l, mix_h, w_first, w_second, w_output, c_in, c_mid, c_out,
         recon, bits_out, part, ups, second, third, fourth,
     ) = refs[n:]
     lat, lon = lax.axis_index("lat"), lax.axis_index("lon")
@@ -256,7 +261,6 @@
     wide = width_of(cols_dev)
     deep = SUB * ch
     reach = (SUB + 2) * ch
-    stride = taps.shape[0] // 9
 
     lane_ch = iota((ch, deep), 1)
     fold = one_hot(lane_ch - ch * div_24(lane_ch) == iota((ch, deep), 0))
@@ -283,25 +287,23 @@
 
     t_levels = row_inside(mix_l[...])
     t_hidden = block_diagonal(mix_h[...])
-    a_in = [row_inside(p) for p in parts(c_in[...], 2)]
-    a_mid = [block_diagonal(p) for p in parts(c_mid[...], 2)]
-    a_out = [rows_out(p) for p in parts(c_out[...], 2)]
+    a_in = jnp.concatenate([row_inside(p) for p in parts(c_in[...], 2)], 0)
+    a_in = jnp.concatenate([a_in, a_in], 1)
+    a_mid = jnp.concatenate([block_diagonal(p) for p in parts(c_mid[...], 2)], 0)
+    a_out = jnp.concatenate([rows_out(p) for p in parts(c_out[...], 2)], 0)
 
     lane_re = iota((ch, reach), 1)
     fold_re = one_hot(lane_re - ch * div_24(lane_re) == iota((ch, reach), 0))
-    wide_taps = dot(taps[...], fold_re)
     step = div_24(iota((deep, reach), 1)) - div_24(iota((deep, reach), 0))
     step_out = div_24(iota((bands * SUB, reach), 1)) - (iota((bands * SUB, reach), 0) & 7)
 
-    def conv_taps(first_row):
+    def conv_taps(w):
+        grown = [[dot(w[a, b], fold_re) for b in range(3)] for a in range(3)]
         out = []
         for b in range(3):
             total = jnp.zeros((deep, reach), F32)
             for a in range(3):
-                at = (3 * a + b) * stride + first_row
-                total = jnp.where(
-                    step == a, jnp.concatenate([wide_taps[at : at + ch]] * SUB, 0), total
-                )
+                total = jnp.where(step == a, jnp.concatenate([grown[a][b]] * SUB, 0), total)
             out.append(total.astype(BF))
         return jnp.concatenate(out, 0)
 
@@ -310,10 +312,10 @@
         for b in range(3):
             total = jnp.zeros((bands * SUB, reach), F32)
             for a in range(3):
-                at = (3 * a + b) * stride + 2 * ch
+                one = dot(w_output[a, b], fold_re)
                 grown = jnp.concatenate(
                     [
-                        jnp.broadcast_to(wide_taps[at + o : at + o + 1], (SUB, reach))
+                        jnp.broadcast_to(one[o : o + 1], (SUB, reach))
                         for o in range(bands)
                     ],
                     0,
@@ -322,8 +324,8 @@
             out.append(total)
         return jnp.concatenate(out, 0).astype(BF)
 
-    t_first = conv_taps(0)
-    t_second = conv_taps(ch)
+    t_first = conv_taps(w_first)
+    t_second = conv_taps(w_second)
     t_output = output_taps()
 
     tall_up = ups.shape[1]
@@ -437,30 +439,47 @@
         scale = anchor[level]
         odd = lat * rows + lon * cols + parity[level]
 
-        def rate_step(g, total, level=level, rows=rows, cols=cols, e=e, cover=cover, full=full, scale=scale, odd=odd):
-            window = e[pl.ds(aligned(g * SUB, SUB), 3 * SUB), :]
-            moved = {i: window[SUB + i : 2 * SUB + i] for i in range(-2, 3)}
-            context = [
-                (moved[i] if j == 0 else pltpu.roll(moved[i], (-j) % full, 1))[:, :cover]
-                for i, j in context_steps
-            ]
-            inner = jnp.maximum(dot_pairs(a_in, jnp.concatenate(context, 0)), 0.0)
+        blocks = 2 if rows % (2 * SUB) == 0 else 1
+
+        def rate_step(g, total, blocks=blocks, level=level, rows=rows, cols=cols, e=e, cover=cover, full=full, scale=scale, odd=odd):
+            def context_of(block):
+                window = e[pl.ds(aligned(block * SUB, SUB), 3 * SUB), :]
+                moved = {i: window[SUB + i : 2 * SUB + i] for i in range(-2, 3)}
+                near = [
+                    (moved[i] if j == 0 else pltpu.roll(moved[i], (-j) % full, 1))[:, :cover]
+                    for i, j in context_steps
+                ]
+                return near, moved[0][:, :cover]
+
+            row, col = iota((SUB, cover), 0), iota((SUB, cover), 1)
+            first = ((row + col + odd) & 1) == 0
+            near, here = context_of(g * blocks)
+            cells = [here]
+            if blocks == 2:
+                later, here = context_of(g * blocks + 1)
+                cells.append(here)
+                near = [
+                    jnp.where(first, pltpu.roll(q, cover - 1, 1), p) for p, q in zip(near, later)
+                ]
+            inner = jnp.maximum(dot_pairs(a_in, jnp.concatenate(near, 0)), 0.0)
             outer = jnp.maximum(dot_pairs(a_mid, inner), 0.0)
             raw = dot_pairs(a_out, outer)
             mu, sigma = raw[:SUB], raw[SUB:]
-            row, col = iota((SUB, cover), 0), iota((SUB, cover), 1)
-            first = ((row + col + odd) & 1) == 0
-            centre = jnp.where(first, 0.0, mu)
-            soft = jnp.maximum(sigma, 0.0) + jnp.log1p(jnp.exp(-jnp.abs(sigma)))
-            spread = jnp.where(first, scale, 0.1 + soft)
-            bits = laplace_bits(moved[0][:, :cover] - centre, spread)
-            if level == 0:
-                bits_out[pl.ds(aligned(g * SUB, SUB), SUB), :] = bits
-            if rows < SUB or cols < LANES:
-                bits = jnp.where((row < rows) & (col < cols), bits, 0.0)
-            return total + bits
-
-        total = looped(max(1, rows // SUB), 4, rate_step, jnp.zeros((SUB, cover), F32))
+            soft = 0.1 + jnp.maximum(sigma, 0.0) + jnp.log1p(jnp.exp(-jnp.abs(sigma)))
+            for k, here in enumerate(cells):
+                if k == 1:
+                    mu, soft = pltpu.roll(mu, 1, 1), pltpu.roll(soft, 1, 1)
+                centre = jnp.where(first, 0.0, mu)
+                spread = jnp.where(first, scale, soft)
+                bits = laplace_bits(here - centre, spread)
+                if level == 0:
+                    bits_out[pl.ds(aligned((g * blocks + k) * SUB, SUB), SUB), :] = bits
+                if rows < SUB or cols < LANES:
+                    bits = jnp.where((row < rows) & (col < cols), bits, 0.0)
+                total = total + bits
+            return total
+
+        total = looped(max(1, rows // (SUB * blocks)), 2, rate_step, jnp.zeros((SUB, cover), F32))
         sums = put(sums, 1 + level, jnp.sum(total))
     part[...] = sums
 
@@ -498,8 +517,7 @@
         ),
         name="halo",
     )(tile_seeds, *latents)
-    taps = jnp.concatenate([conv_first, conv_second, conv_output], 0).transpose(2, 3, 0, 1)
-    taps = jnp.pad(taps, ((0, 0), (0, 0), (0, -taps.shape[2] % SUB), (0, 0))).reshape(-1, ch)
+    convs = [w.transpose(2, 3, 0, 1) for w in (conv_first, conv_second, conv_output)]
     wide = wides[0]
     tall_up = rows_dev + SUB
     recon, bits, part = pl.pallas_call(
@@ -509,7 +527,7 @@
             jax.ShapeDtypeStruct((rows_dev, cols_dev), F32),
             jax.ShapeDtypeStruct((2 * SUB, LANES), F32),
         ],
-        in_specs=[vmem] * (n + 1) + [smem] * 2 + [vmem] * 6,
+        in_specs=[vmem] * (n + 1) + [smem] * 2 + [vmem] * 8,
         out_specs=[vmem] * 3,
         scratch_shapes=[
             pltpu.VMEM((n, tall_up, wide), F32),
@@ -521,7 +539,7 @@
         name="step",
     )(
         *extended, target, anchor_parity, anchor_scale, mix_levels, mix_hidden,
-        taps, context_in, context_mid, context_out,
+        *convs, context_in, context_mid, context_out,
     )
     lats, lons = lax.axis_size("lat"), lax.axis_size("lon")
     total = pl.pallas_call(

time: 56.8 us -> 53.8 us (0.947)
  Pallas kernels: 48.7 us -> 45.2 us
  local copies, waits for them, and re-layouts: 5.64 us -> 6.21 us
    pallas_call x1, Pallas kernels: 27.4 us -> 24 us  [local(): pl.pallas_call(functools.partial(local_kernel, shapes, ch, bands, pixel_c...]
    unnamed x38 -> x33, local copies, waits for them, and re-layouts: 4.92 us -> 5.52 us
where the time goes in v3:
time: 53.8 us; the launch traced here: 53.4 us
  Pallas kernels  45.2 us (84%)
  local copies, waits for them, and re-layouts  6.21 us (12%)
  between operations  1.42 us (3%)
    pallas_call x1, Pallas kernels, local(): pl.pallas_call(functools.partial(local_kernel, shapes, ch, bands, pixel_c...  24 us
    pallas_call x1, Pallas kernels, local(): pl.pallas_call(functools.partial(halo_kernel, shapes), out_shape=[jax.Sha...  12.5 us
    pallas_call x1, Pallas kernels, local(): pl.pallas_call(sum_kernel, out_shape=jax.ShapeDtypeStruct(part.shape, F32...  8.65 us
    unnamed x33, local copies, waits for them, and re-layouts  5.52 us

profile of v3, /device:TPU:0, one launch (start us, length us, event | category | flops | bytes accessed | tf_op | source)
XLA Modules:
  0.0 53.4 jit_solution(17447083985998277556)
XLA Ops:
  0.6 0.0 copy-start.4
  1.3 0.8 %copy.24.refs_9_ = bf16[24,6]{1,0:T(8,128)(2,1)S(1)} copy(bf16[24,6]{0,1:T(8,128)(2,1)} %param.29) | data formatting | bytes 576 | tf_op args[10]
  2.1 0.7 %copy.30 = bf16[3,24,3,3]{1,0,3,2:T(4,128)(2,1)S(1)} copy(bf16[3,24,3,3]{1,3,2,0:T(4,128)(2,1)} %param.33) | data formatting | bytes 2592 | tf_op args[14]
  2.8 0.0 copy-start.10
  2.8 0.8 %copy.25.refs_14_ = f32[24,12]{1,0:T(8,128)S(1)} copy(f32[24,12]{0,1:T(8,128)} %param.34) | data formatting | bytes 2304 | tf_op args[15]
  3.6 0.0 copy-done.4
  3.6 0.0 copy-start.1
  3.7 0.9 %copy-done.1 = f32[64,512]{1,0:T(8,128)S(1)} copy-done((f32[64,512]{1,0:T(8,128)S(1)}, f32[64,512]{1,0:T(8,128)}, u32[]{:S(2)}) %copy-start.1) | copy-done | bytes 131096
  4.6 12.5 %halo.1 = (f32[80,640]{1,0:T(8,128)S(1)}, f32[48,384]{1,0:T(8,128)S(1)}, f32[32,256]{1,0:T(8,128)S(1)}, f32[24,128]{1,0:T(8,128)S(1)}, f32[24,128]{1,0:T(8,128)S(1)}, /*index=5*/f32[24,128]{1,0:T(8,128)S(1)}) custom-call(s32[1,1]{1,0:T(1,128)S(6)} %copy.31.seed_ref, f32[64,512]{1,0:T(8,128)S(1)} %copy-done.1, f32[32,256]{1,0:T(8,128)S(1)} %copy-done.4, ...), custom_call_target="tpu_custom_call" | custom-call | tf_op jit(solution)/shard_map/halo/pallas_call | solution.py:505
  17.1 0.0 copy-start.7
  17.1 0.0 copy-start.13
  17.1 0.0 copy-start.11
  17.1 0.0 copy-start.12
  17.2 0.6 %copy-done.7 = bf16[24,24]{1,0:T(8,128)(2,1)S(1)} copy-done((bf16[24,24]{1,0:T(8,128)(2,1)S(1)}, bf16[24,24]{1,0:T(8,128)(2,1)}, u32[]{:S(2)}) %copy-start.7) | copy-done | bytes 1176
  17.8 0.0 copy-done.11
  17.8 0.0 copy-done.12
  17.8 1.0 %copy-done = f32[3,64,512]{2,1,0:T(8,128)S(1)} copy-done((f32[3,64,512]{2,1,0:T(8,128)S(1)}, f32[3,64,512]{2,1,0:T(8,128)}, u32[]{:S(2)}) %copy-start) | copy-done | bytes 393240
  18.8 24.0 %step.1 = (f32[3,64,512]{2,1,0:T(8,128)}, f32[64,512]{1,0:T(8,128)}, f32[16,128]{1,0:T(8,128)S(1)}) custom-call(f32[80,640]{1,0:T(8,128)S(1)} %get-tuple-element.13.refs_0_, f32[48,384]{1,0:T(8,128)S(1)} %get-tuple-element.14.refs_1_, f32[32,256]{1,0:T(8,128)S(1)} %get-tuple-element.15.refs_2_, f32[24,128]{1,0:T(8,128)S(1)} %get-tuple-element.16.refs_3_, ...), custom_call_target="tpu_custom_call" | custom-call | tf_op jit(solution)/shard_map/step/pallas_call | solution.py:523
  42.8 8.7 %sums.1 = f32[16,128]{1,0:T(8,128)S(1)} custom-call(f32[16,128]{1,0:T(8,128)S(1)} %get-tuple-element.21.part), custom_call_target="tpu_custom_call" | custom-call | tf_op jit(solution)/shard_map/sums/pallas_call | solution.py:545
  51.5 0.0 copy-start.14
  51.5 0.6 %copy-done.14 = f32[1,7]{1,0:T(1,128)S(1)} copy-done((f32[1,7]{1,0:T(1,128)S(1)}, f32[1,7]{1,0:T(1,128)}, u32[]{:S(2)}) %copy-start.14) | copy-done | bytes 52
  52.2 0.5 multiply_bitcast_fusion
  52.7 0.1 reshape.11
  52.8 0.6 %copy.29 = f32[3,3,3,24]{3,0,2,1:T(4,128)} copy(f32[3,3,3,24]{3,2,1,0:T(4,128)S(1)} %reshape.11) | data formatting | bytes 5184 | tf_op jit(solution)/shard_map/reshape | solution.py:561
  (15 shorter events, 0.0 us)
Async XLA Ops:
  0.6 3.0 %copy-start.4 = (f32[32,256]{1,0:T(8,128)S(1)}, f32[32,256]{1,0:T(8,128)}, u32[]{:S(2)}) copy-start(f32[32,256]{1,0:T(8,128)} %refs_1_.1) | copy-start | bytes 98308
  2.8 0.8 %copy-start.6 = (f32[16,128]{1,0:T(8,128)S(1)}, f32[16,128]{1,0:T(8,128)}, u32[]{:S(2)}) copy-start(f32[16,128]{1,0:T(8,128)} %refs_2_.1) | copy-start | bytes 24580
  2.8 0.8 %copy-start.8 = (f32[8,64]{1,0:T(8,128)S(1)}, f32[8,64]{1,0:T(8,128)}, u32[]{:S(2)}) copy-start(f32[8,64]{1,0:T(8,128)} %refs_3_.1) | copy-start | bytes 6148
  2.8 0.8 %copy-start.9 = (f32[4,32]{1,0:T(4,128)S(1)}, f32[4,32]{1,0:T(4,128)}, u32[]{:S(2)}) copy-start(f32[4,32]{1,0:T(4,128)} %refs_4_.1) | copy-start | bytes 1540
  2.8 0.8 %copy-start.10 = (f32[2,16]{1,0:T(2,128)S(1)}, f32[2,16]{1,0:T(2,128)}, u32[]{:S(2)}) copy-start(f32[2,16]{1,0:T(2,128)} %refs_5_.1) | copy-start | bytes 388
  3.6 0.9 %copy-start.1 = (f32[64,512]{1,0:T(8,128)S(1)}, f32[64,512]{1,0:T(8,128)}, u32[]{:S(2)}) copy-start(f32[64,512]{1,0:T(8,128)} %refs_0_.1) | copy-start | bytes 393220
  4.5 12.6 %copy-start.2 = (bf16[24,24,3,3]{1,0,3,2:T(8,128)(2,1)S(1)}, bf16[24,24,3,3]{1,0,3,2:T(8,128)(2,1)}, u32[]{:S(2)}) copy-start(bf16[24,24,3,3]{1,0,3,2:T(8,128)(2,1)} %param.31) | copy-start | bytes 31108
  4.5 12.6 %copy-start.3 = (bf16[24,24,3,3]{1,0,3,2:T(8,128)(2,1)S(1)}, bf16[24,24,3,3]{1,0,3,2:T(8,128)(2,1)}, u32[]{:S(2)}) copy-start(bf16[24,24,3,3]{1,0,3,2:T(8,128)(2,1)} %param.32) | copy-start | bytes 31108
  4.6 12.6 %copy-start.5 = (f32[24,24]{1,0:T(8,128)S(1)}, f32[24,24]{1,0:T(8,128)}, u32[]{:S(2)}) copy-start(f32[24,24]{1,0:T(8,128)} %refs_15_.1) | copy-start | bytes 6916
  17.1 0.7 %copy-start.7 = (bf16[24,24]{1,0:T(8,128)(2,1)S(1)}, bf16[24,24]{1,0:T(8,128)(2,1)}, u32[]{:S(2)}) copy-start(bf16[24,24]{1,0:T(8,128)(2,1)} %refs_10_.1) | copy-start | bytes 3460
  17.1 0.7 %copy-start.13 = (f32[6]{0:T(128)S(1)}, f32[6]{0:T(128)}, u32[]{:S(2)}) copy-start(f32[6]{0:T(128)} %refs_8_.1) | copy-start | bytes 76
  17.1 0.7 %copy-start.11 = (f32[2,24]{1,0:T(2,128)S(1)}, f32[2,24]{1,0:T(2,128)}, u32[]{:S(2)}) copy-start(f32[2,24]{1,0:T(2,128)} %refs_16_.1) | copy-start | bytes 580
  17.1 0.7 %copy-start.12 = (s32[6]{0:T(128)S(1)}, s32[6]{0:T(128)}, u32[]{:S(2)}) copy-start(s32[6]{0:T(128)} %refs_7_.1) | copy-start | bytes 76
  17.8 1.0 %copy-start = (f32[3,64,512]{2,1,0:T(8,128)S(1)}, f32[3,64,512]{2,1,0:T(8,128)}, u32[]{:S(2)}) copy-start(f32[3,64,512]{2,1,0:T(8,128)} %refs_6_.1) | copy-start | bytes 1179652
  51.5 0.7 %copy-start.14 = (f32[1,7]{1,0:T(1,128)S(1)}, f32[1,7]{1,0:T(1,128)}, u32[]{:S(2)}) copy-start(f32[1,7]{1,0:T(1,128)} %constant.6) | copy-start | bytes 88

commit v4 on v3

--- a/solution.py
+++ b/solution.py
@@ -199,6 +199,10 @@
     return out
 
 
+def dot_first(a, b):
+    return lax.dot_general(a, b, (((0,), (0,)), ((), ())), preferred_element_type=F32)
+
+
 def dot_pairs(a, x):
     hi, lo = parts(x, 2)
     m, k = a.shape[0] // 2, a.shape[1]
@@ -270,11 +274,11 @@
         return jnp.where(same_row, jnp.concatenate([dot(w, fold)] * SUB, 0), 0.0).astype(BF)
 
     def row_inside(w):
-        k = w.shape[1]
+        k = w.shape[0]
         spread = one_hot((iota((k, k * SUB), 1) >> 3) == iota((k, k * SUB), 0))
         shape = (deep, k * SUB)
         keep = (iota(shape, 1) & 7) == div_24(iota(shape, 0))
-        return jnp.where(keep, jnp.concatenate([dot(w, spread)] * SUB, 0), 0.0).astype(BF)
+        return jnp.where(keep, jnp.concatenate([dot_first(w, spread)] * SUB, 0), 0.0).astype(BF)
 
     def rows_out(w):
         wide_w = dot(w, fold)
@@ -308,14 +312,14 @@
         return jnp.concatenate(out, 0)
 
     def output_taps():
+        grown_out = [[dot(w_output[o, a], fold_re) for a in range(3)] for o in range(bands)]
         out = []
         for b in range(3):
             total = jnp.zeros((bands * SUB, reach), F32)
             for a in range(3):
-                one = dot(w_output[a, b], fold_re)
                 grown = jnp.concatenate(
                     [
-                        jnp.broadcast_to(one[o : o + 1], (SUB, reach))
+                        jnp.broadcast_to(grown_out[o][a][b : b + 1], (SUB, reach))
                         for o in range(bands)
                     ],
                     0,
@@ -409,29 +413,8 @@
         return squares + error * error, grad
 
     m = bands * SUB
-    squares, grad = looped(
-        rows_dev // SUB,
-        4,
-        output_step,
-        (jnp.zeros((m, cols_dev), F32), jnp.zeros((3 * m, reach), F32)),
-    )
-    pad = -reach % LANES
-    grad = jnp.concatenate([grad, jnp.zeros((3 * m, pad), F32)], 1)
-    line = iota(grad.shape, 0) & 7
-    moved = grad
-    for y in range(1, SUB):
-        moved = jnp.where(line == y, pltpu.roll(grad, reach + pad - y * ch, 1), moved)
-    folded = jnp.sum(moved[:, :LANES].reshape(3 * bands, SUB, LANES), axis=1)
-    sums = jnp.concatenate([folded, jnp.zeros((part.shape[0] - 3 * bands, LANES), F32)], 0)
-
-    shape = part.shape
-    last = iota(shape, 0) == 3 * bands
-
-    def put(sums, lane, value):
-        return jnp.where(last & (iota(shape, 1) == lane), value, sums)
-
-    sums = put(sums, 0, jnp.sum(squares))
-
+    totals = []
+    m = bands * SUB
     for level, (rows, cols) in enumerate(shapes):
         e = ext[level]
         cover = max(cols, LANES)
@@ -479,8 +462,40 @@
                 total = total + bits
             return total
 
-        total = looped(max(1, rows // (SUB * blocks)), 2, rate_step, jnp.zeros((SUB, cover), F32))
-        sums = put(sums, 1 + level, jnp.sum(total))
+        count = max(1, rows // (SUB * blocks))
+        start = jnp.zeros((SUB, cover), F32)
+        if level == 0:
+
+            def both_steps(g, carry):
+                out, total = carry
+                for k in range(blocks):
+                    out = output_step(g * blocks + k, out)
+                return out, rate_step(g, total)
+
+            start_out = (jnp.zeros((m, cols_dev), F32), jnp.zeros((3 * m, reach), F32))
+            (squares, grad), total = looped(count, 2, both_steps, (start_out, start))
+        else:
+            total = looped(count, 2, rate_step, start)
+        totals.append(jnp.sum(total) * (1.0 / (rows * cols * lats * lax.axis_size("lon"))))
+    pad = -reach % LANES
+    grad = jnp.concatenate([grad, jnp.zeros((3 * m, pad), F32)], 1)
+    line = iota(grad.shape, 0) & 7
+    moved = grad
+    for y in range(1, SUB):
+        moved = jnp.where(line == y, pltpu.roll(grad, reach + pad - y * ch, 1), moved)
+    folded = jnp.sum(moved[:, :LANES].reshape(3 * bands, SUB, LANES), axis=1)
+    sums = jnp.concatenate([folded, jnp.zeros((part.shape[0] - 3 * bands, LANES), F32)], 0)
+
+    shape = part.shape
+    last = iota(shape, 0) == 3 * bands
+
+    def put(sums, lane, value):
+        return jnp.where(last & (iota(shape, 1) == lane), value, sums)
+
+    sums = put(sums, 0, jnp.sum(squares) * (1.0 / pixel_count))
+
+    for level, value in enumerate(totals):
+        sums = put(sums, 1 + level, value)
     part[...] = sums
 
 
@@ -517,7 +532,8 @@
         ),
         name="halo",
     )(tile_seeds, *latents)
-    convs = [w.transpose(2, 3, 0, 1) for w in (conv_first, conv_second, conv_output)]
+    convs = [w.transpose(2, 3, 0, 1) for w in (conv_first, conv_second)]
+    convs.append(conv_output.transpose(0, 2, 3, 1))
     wide = wides[0]
     tall_up = rows_dev + SUB
     recon, bits, part = pl.pallas_call(
@@ -538,8 +554,8 @@
         compiler_params=pltpu.CompilerParams(vmem_limit_bytes=48 * 2**20),
         name="step",
     )(
-        *extended, target, anchor_parity, anchor_scale, mix_levels, mix_hidden,
-        *convs, context_in, context_mid, context_out,
+        *extended, target, anchor_parity, anchor_scale, mix_levels.T, mix_hidden,
+        *convs, context_in.T, context_mid, context_out,
     )
     lats, lons = lax.axis_size("lat"), lax.axis_size("lon")
     total = pl.pallas_call(
@@ -559,10 +575,7 @@
         name="sums",
     )(part)
     grad = total[: 3 * bands, : 3 * ch].reshape(3, bands, 3, ch).transpose(1, 3, 2, 0)
-    counts = jnp.array(
-        [pixel_count] + [float(r * c * devices) for r, c in shapes], dtype=F32
-    )
-    loss_terms = total[3 * bands, : n + 1] / counts
+    loss_terms = total[3 * bands, : n + 1]
     return (recon, bits, loss_terms, grad)
 
 

time: 53.8 us -> 50.9 us (0.946)
  Pallas kernels: 45.2 us -> 43.2 us
    pallas_call x1, Pallas kernels: 24 us -> 21.9 us  [local(): pl.pallas_call(functools.partial(local_kernel, shapes, ch, bands, pixel_c...]
    unnamed x33 -> x34, local copies, waits for them, and re-layouts: 5.52 us -> 4.67 us
where the time goes in v4:
time: 50.9 us; the launch traced here: 50.5 us
  Pallas kernels  43.2 us (85%)
  local copies, waits for them, and re-layouts  5.87 us (12%)
  between operations  1.46 us (3%)
    pallas_call x1, Pallas kernels, local(): pl.pallas_call(functools.partial(local_kernel, shapes, ch, bands, pixel_c...  21.9 us
    pallas_call x1, Pallas kernels, local(): pl.pallas_call(functools.partial(halo_kernel, shapes), out_shape=[jax.Sha...  12.6 us
    pallas_call x1, Pallas kernels, local(): pl.pallas_call(sum_kernel, out_shape=jax.ShapeDtypeStruct(part.shape, F32...  8.67 us
    unnamed x34, local copies, waits for them, and re-layouts  4.67 us

profile of v4, /device:TPU:0, one launch (start us, length us, event | category | flops | bytes accessed | tf_op | source)
XLA Modules:
  0.0 50.5 jit_solution(9584199671456326082)
XLA Ops:
  0.6 0.0 copy-start.8
  1.3 0.0 copy-start.11
  1.3 0.0 copy-start.13
  1.3 0.0 copy-done.8
  1.3 0.7 %copy-done.11 = f32[4,32]{1,0:T(4,128)S(1)} copy-done((f32[4,32]{1,0:T(4,128)S(1)}, f32[4,32]{1,0:T(4,128)}, u32[]{:S(2)}) %copy-start.11) | copy-done | bytes 536
  2.0 0.0 copy-done.13
  2.0 0.9 %copy-done.1 = f32[64,512]{1,0:T(8,128)S(1)} copy-done((f32[64,512]{1,0:T(8,128)S(1)}, f32[64,512]{1,0:T(8,128)}, u32[]{:S(2)}) %copy-start.1) | copy-done | bytes 131096
  2.9 0.8 %copy-done.4 = f32[32,256]{1,0:T(8,128)S(1)} copy-done((f32[32,256]{1,0:T(8,128)S(1)}, f32[32,256]{1,0:T(8,128)}, u32[]{:S(2)}) %copy-start.4) | copy-done | bytes 32792
  3.7 0.7 %copy-done.10 = f32[8,64]{1,0:T(8,128)S(1)} copy-done((f32[8,64]{1,0:T(8,128)S(1)}, f32[8,64]{1,0:T(8,128)}, u32[]{:S(2)}) %copy-start.10) | copy-done | bytes 2072
  4.4 0.0 copy-start.9
  4.4 0.0 copy-start.14
  4.4 0.0 copy-start.15
  4.4 0.0 copy-start.16
  4.4 12.6 %halo.1 = (f32[80,640]{1,0:T(8,128)S(1)}, f32[48,384]{1,0:T(8,128)S(1)}, f32[32,256]{1,0:T(8,128)S(1)}, f32[24,128]{1,0:T(8,128)S(1)}, f32[24,128]{1,0:T(8,128)S(1)}, /*index=5*/f32[24,128]{1,0:T(8,128)S(1)}) custom-call(s32[1,1]{1,0:T(1,128)S(6)} %copy.25.seed_ref, f32[64,512]{1,0:T(8,128)S(1)} %copy-done.1, f32[32,256]{1,0:T(8,128)S(1)} %copy-done.4, ...), custom_call_target="tpu_custom_call" | custom-call | tf_op jit(solution)/shard_map/halo/pallas_call | solution.py:520
  17.0 0.0 copy-start.6
  17.0 0.0 copy-start.12
  17.0 0.0 copy-done.2
  17.1 0.6 %copy-done.6 = bf16[3,24,3,3]{1,3,2,0:T(4,128)(2,1)S(1)} copy-done((bf16[3,24,3,3]{1,3,2,0:T(4,128)(2,1)S(1)}, bf16[3,24,3,3]{1,3,2,0:T(4,128)(2,1)}, u32[]{:S(2)}) %copy-start.6) | copy-done | bytes 1320
  17.7 1.0 %copy-done = f32[3,64,512]{2,1,0:T(8,128)S(1)} copy-done((f32[3,64,512]{2,1,0:T(8,128)S(1)}, f32[3,64,512]{2,1,0:T(8,128)}, u32[]{:S(2)}) %copy-start) | copy-done | bytes 393240
  18.7 21.9 %step.1 = (f32[3,64,512]{2,1,0:T(8,128)}, f32[64,512]{1,0:T(8,128)}, f32[16,128]{1,0:T(8,128)S(1)}) custom-call(f32[80,640]{1,0:T(8,128)S(1)} %get-tuple-element.13.refs_0_, f32[48,384]{1,0:T(8,128)S(1)} %get-tuple-element.14.refs_1_, f32[32,256]{1,0:T(8,128)S(1)} %get-tuple-element.15.refs_2_, f32[24,128]{1,0:T(8,128)S(1)} %get-tuple-element.16.refs_3_, ...), custom_call_target="tpu_custom_call" | custom-call | tf_op jit(solution)/shard_map/step/pallas_call | solution.py:539
  40.6 8.7 %sums.1 = f32[16,128]{1,0:T(8,128)S(1)} custom-call(f32[16,128]{1,0:T(8,128)S(1)} %get-tuple-element.21.part), custom_call_target="tpu_custom_call" | custom-call | tf_op jit(solution)/shard_map/sums/pallas_call | solution.py:561
  49.3 0.5 %slice_bitcast_fusion = f32[7]{0:T(128)} fusion(f32[16,128]{1,0:T(8,128)S(1)} %sums.1), kind=kLoop, calls=%fused_computation.1 | loop fusion | bytes 56 | tf_op jit(solution)/shard_map/squeeze | solution.py:578
  49.8 0.1 reshape.11
  49.9 0.6 %copy.24 = f32[3,3,3,24]{3,0,2,1:T(4,128)} copy(f32[3,3,3,24]{3,2,1,0:T(4,128)S(1)} %reshape.11) | data formatting | bytes 5184 | tf_op jit(solution)/shard_map/reshape | solution.py:577
  (16 shorter events, 0.0 us)
Async XLA Ops:
  0.6 0.7 %copy-start.8 = (f32[16,128]{1,0:T(8,128)S(1)}, f32[16,128]{1,0:T(8,128)}, u32[]{:S(2)}) copy-start(f32[16,128]{1,0:T(8,128)} %refs_2_.1) | copy-start | bytes 24580
  1.3 0.7 %copy-start.11 = (f32[4,32]{1,0:T(4,128)S(1)}, f32[4,32]{1,0:T(4,128)}, u32[]{:S(2)}) copy-start(f32[4,32]{1,0:T(4,128)} %refs_4_.1) | copy-start | bytes 1540
  1.3 0.7 %copy-start.13 = (f32[2,16]{1,0:T(2,128)S(1)}, f32[2,16]{1,0:T(2,128)}, u32[]{:S(2)}) copy-start(f32[2,16]{1,0:T(2,128)} %refs_5_.1) | copy-start | bytes 388
  2.0 0.9 %copy-start.1 = (f32[64,512]{1,0:T(8,128)S(1)}, f32[64,512]{1,0:T(8,128)}, u32[]{:S(2)}) copy-start(f32[64,512]{1,0:T(8,128)} %refs_0_.1) | copy-start | bytes 393220
  2.9 0.8 %copy-start.4 = (f32[32,256]{1,0:T(8,128)S(1)}, f32[32,256]{1,0:T(8,128)}, u32[]{:S(2)}) copy-start(f32[32,256]{1,0:T(8,128)} %refs_1_.1) | copy-start | bytes 98308
  3.7 0.7 %copy-start.10 = (f32[8,64]{1,0:T(8,128)S(1)}, f32[8,64]{1,0:T(8,128)}, u32[]{:S(2)}) copy-start(f32[8,64]{1,0:T(8,128)} %refs_3_.1) | copy-start | bytes 6148
  4.4 12.7 %copy-start.2 = (bf16[24,24,3,3]{1,0,3,2:T(8,128)(2,1)S(1)}, bf16[24,24,3,3]{1,0,3,2:T(8,128)(2,1)}, u32[]{:S(2)}) copy-start(bf16[24,24,3,3]{1,0,3,2:T(8,128)(2,1)} %param.30) | copy-start | bytes 31108
  4.4 12.7 %copy-start.3 = (bf16[24,24,3,3]{1,0,3,2:T(8,128)(2,1)S(1)}, bf16[24,24,3,3]{1,0,3,2:T(8,128)(2,1)}, u32[]{:S(2)}) copy-start(bf16[24,24,3,3]{1,0,3,2:T(8,128)(2,1)} %param.31) | copy-start | bytes 31108
  4.4 12.7 %copy-start.5 = (f32[24,24]{1,0:T(8,128)S(1)}, f32[24,24]{1,0:T(8,128)}, u32[]{:S(2)}) copy-start(f32[24,24]{1,0:T(8,128)} %refs_15_.1) | copy-start | bytes 6916
  4.4 12.7 %copy-start.7 = (f32[24,12]{0,1:T(8,128)S(1)}, f32[24,12]{0,1:T(8,128)}, u32[]{:S(2)}) copy-start(f32[24,12]{0,1:T(8,128)} %param.33) | copy-start | bytes 3460
  4.4 12.7 %copy-start.9 = (bf16[24,24]{1,0:T(8,128)(2,1)S(1)}, bf16[24,24]{1,0:T(8,128)(2,1)}, u32[]{:S(2)}) copy-start(bf16[24,24]{1,0:T(8,128)(2,1)} %refs_10_.1) | copy-start | bytes 3460
  4.4 12.7 %copy-start.14 = (f32[2,24]{1,0:T(2,128)S(1)}, f32[2,24]{1,0:T(2,128)}, u32[]{:S(2)}) copy-start(f32[2,24]{1,0:T(2,128)} %refs_16_.1) | copy-start | bytes 580
  4.4 12.7 %copy-start.15 = (s32[6]{0:T(128)S(1)}, s32[6]{0:T(128)}, u32[]{:S(2)}) copy-start(s32[6]{0:T(128)} %refs_7_.1) | copy-start | bytes 76
  4.4 12.7 %copy-start.16 = (f32[6]{0:T(128)S(1)}, f32[6]{0:T(128)}, u32[]{:S(2)}) copy-start(f32[6]{0:T(128)} %refs_8_.1) | copy-start | bytes 76
  17.0 0.7 %copy-start.6 = (bf16[3,24,3,3]{1,3,2,0:T(4,128)(2,1)S(1)}, bf16[3,24,3,3]{1,3,2,0:T(4,128)(2,1)}, u32[]{:S(2)}) copy-start(bf16[3,24,3,3]{1,3,2,0:T(4,128)(2,1)} %param.32) | copy-start | bytes 3892
  17.0 0.7 %copy-start.12 = (bf16[24,6]{0,1:T(8,128)(2,1)S(1)}, bf16[24,6]{0,1:T(8,128)(2,1)}, u32[]{:S(2)}) copy-start(bf16[24,6]{0,1:T(8,128)(2,1)} %param.28) | copy-start | bytes 868
  17.7 1.0 %copy-start = (f32[3,64,512]{2,1,0:T(8,128)S(1)}, f32[3,64,512]{2,1,0:T(8,128)}, u32[]{:S(2)}) copy-start(f32[3,64,512]{2,1,0:T(8,128)} %refs_6_.1) | copy-start | bytes 1179652
